TPU v7x, 256 devices: a whole 4x4x8 slice. The times are simulated.
256 devices in a mesh: sec: 2 (over core), tm: 32 (over z, y), dp: 4 (over x).
Axes of the slice: x: 4, y: 4, z: 8, core: 2. Of those that a mesh axis runs over, the one named last changes fastest.
Arguments:
- enc_input: bfloat16 [4, 32768, 1024], P('dp', ('sec', 'tm')), may hold values from -6 to 6
- llm_grads: bfloat16 [4, 65536, 1024], P('dp', ('sec', 'tm')), may hold values from -6 to 6
- slot_block: int32 [4, 4096], P('dp', ('sec', 'tm')), may hold values from -1 to 2047, as said below
- utt_lengths: int32 [4, 262], P('dp'), may hold values from 1 to 250, 32768 in all within a row
- ln_gain: float32 [1024], replicated, may hold values from 0.1 to 1.9
- ln_bias: float32 [1024], replicated, may hold values from -3 to 3
- w_in: bfloat16 [1024, 2048], replicated, may hold values from -0.1875 to 0.1875
- dw_kernel: float32 [9, 1024], replicated, may hold values from -2 to 2
- bn_gain: float32 [1024], replicated, may hold values from 0.1 to 1.9
- bn_bias: float32 [1024], replicated, may hold values from -3 to 3
- w_out: bfloat16 [1024, 1024], replicated, may hold values from -0.1875 to 0.1875
Outputs:
- grad_input: bfloat16 [4, 32768, 1024], P('dp', ('sec', 'tm'))
Inputs may be any that keep to these rules, and one draw needn't show every extreme that they name: `slot_block`: in each group every block 0 to 2047 stands in exactly one slot and the other slots hold -1; block b holds the timeline frames b * 16 to b * 16 + 15. The 64 slots of one device hold at most 1 block of any one timeline device, and for every timeline device some device's slots hold exactly 1 of its blocks. `utt_lengths`: each group's lengths sum to 32768, and the largest is 250.
All inputs are finite; a program needn't handle non-finite values.
Results may differ from a plain program's by a relative error of at most 0.0048.
Values may be sent and summed in bfloat16 or wider, within the bound.
A program may use at most 64 MiB of HBM per device.

v0:
```python
import jax
import jax.numpy as jnp
from jax import lax
from jax.sharding import PartitionSpec as P

NBE = 32


norm_eps = 1e-05


def extended(block, sides, width):
    for axis, dim in sides:
        count = lax.axis_size(axis)
        forward = [(i, i + 1) for i in range(count - 1)]
        backward = [(target, source) for source, target in forward]
        low = lax.ppermute(
            lax.slice_in_dim(block, block.shape[dim] - width, None, axis=dim), axis, forward
        )
        high = lax.ppermute(lax.slice_in_dim(block, 0, width, axis=dim), axis, backward)
        block = jnp.concatenate([low, block, high], axis=dim)
    return block


def agree_mask(segment, inside, start, count, offset):
    left_rows = slice(start, start + count)
    right_rows = slice(start + offset, start + offset + count)
    both_in = inside[left_rows] & inside[right_rows] & (segment[left_rows] == segment[right_rows])
    return both_in.astype(jnp.float32)[:, None]


def dot_transposed(left_side, weight):
    return lax.dot_general(
        left_side, weight, (((1,), (1,)), ((), ())), preferred_element_type=jnp.float32
    )


def local(
    enc_input,
    llm_grads,
    slot_block,
    utt_lengths,
    ln_gain,
    ln_bias,
    w_in,
    dw_kernel,
    bn_gain,
    bn_bias,
    w_out,
):
    shards = lax.axis_size(("sec", "tm"))
    my_shard = lax.axis_index(("sec", "tm"))
    frames = enc_input.shape[1]
    feat_width = enc_input.shape[2]
    tap_count = dw_kernel.shape[0]
    half_width = (tap_count - 1) // 2
    slot_count = slot_block.shape[1]
    block_rows = frames // NBE
    capacity = 2 * NBE // shards
    slot_ids = slot_block[0]
    destination = jnp.where(slot_ids >= 0, slot_ids // NBE, -1)
    slot_order = jnp.arange(slot_count)
    earlier = slot_order[None, :] < slot_order[:, None]
    rank_in = jnp.sum(
        (earlier & (destination[:, None] == destination[None, :])).astype(jnp.int32), axis=1
    )
    buffer_slot = jnp.arange(shards * capacity)
    pick_matrix = (
        ((buffer_slot // capacity)[:, None] == destination[None, :])
        & ((buffer_slot % capacity)[:, None] == rank_in[None, :])
        & (slot_ids >= 0)[None, :]
    )
    slot_rows = llm_grads[0].reshape(slot_count, block_rows * feat_width)
    packed = jnp.dot(
        pick_matrix.astype(jnp.bfloat16), slot_rows, preferred_element_type=jnp.float32
    ).astype(jnp.bfloat16)
    packed_ids = jnp.sum(pick_matrix.astype(jnp.int32) * (slot_ids + 1)[None, :], axis=1) - 1
    arrived, arrived_ids = (
        lax.all_to_all(
            packed.reshape(shards, capacity, block_rows * feat_width),
            ("sec", "tm"),
            split_axis=0,
            concat_axis=0,
            tiled=True,
        ),
        lax.all_to_all(
            packed_ids.reshape(shards, capacity),
            ("sec", "tm"),
            split_axis=0,
            concat_axis=0,
            tiled=True,
        ),
    )
    local_block = arrived_ids.reshape(-1) - my_shard * NBE
    place_matrix = (jnp.arange(NBE)[:, None] == local_block[None, :]).astype(jnp.bfloat16)
    incoming = (
        jnp.dot(
            place_matrix,
            arrived.reshape(shards * capacity, block_rows * feat_width),
            preferred_element_type=jnp.float32,
        )
        .astype(jnp.bfloat16)
        .reshape(frames, feat_width)
    )
    x_float = enc_input[0].astype(jnp.float32)
    row_mean = jnp.mean(x_float, axis=1, keepdims=True)
    centred = x_float - row_mean
    row_rstd = lax.rsqrt(jnp.mean(centred * centred, axis=1, keepdims=True) + norm_eps)
    x_hat = centred * row_rstd
    normed = (x_hat * ln_gain + ln_bias).astype(jnp.bfloat16)
    mixed_proj = jnp.dot(normed, w_in, preferred_element_type=jnp.float32)
    lin_part = mixed_proj[:, :feat_width]
    gate_part = mixed_proj[:, feat_width:]
    gate_sig = jax.nn.sigmoid(gate_part)
    gated_out = (lin_part * gate_sig).astype(jnp.bfloat16)
    timeline = shards * frames
    positions = my_shard * frames - 2 * half_width + jnp.arange(frames + 4 * half_width)
    utt_ends = jnp.cumsum(utt_lengths[0])
    segment = jnp.sum((positions[:, None] >= utt_ends[None, :]).astype(jnp.int32), axis=1)
    inside = (positions >= 0) & (positions < timeline)
    gated_wide = extended(gated_out, ((("sec", "tm"), 0),), half_width).astype(jnp.float32)
    conv_out = jnp.zeros((frames, feat_width), jnp.float32)
    for tap_idx in range(tap_count):
        conv_out = (
            conv_out
            + dw_kernel[tap_idx]
            * agree_mask(segment, inside, 2 * half_width, frames, tap_idx - half_width)
            * gated_wide[tap_idx : tap_idx + frames]
        )
    all_count = float(frames * lax.axis_size(("sec", "tm", "dp")))
    sum_first, sum_second = lax.psum(
        (jnp.sum(conv_out, axis=0), jnp.sum(conv_out * conv_out, axis=0)), ("sec", "tm", "dp")
    )
    bn_mean = sum_first / all_count
    bn_var = sum_second / all_count - bn_mean * bn_mean
    bn_rstd = lax.rsqrt(bn_var + norm_eps)
    z_hat = (conv_out - bn_mean) * bn_rstd
    pre_act = z_hat * bn_gain + bn_bias
    sig_pre = jax.nn.sigmoid(pre_act)
    back_swish = dot_transposed(incoming, w_out)
    d_pre = back_swish * sig_pre * (1.0 + pre_act * (1.0 - sig_pre))
    sum_grad, sum_cross = lax.psum(
        (jnp.sum(d_pre, axis=0), jnp.sum(d_pre * z_hat, axis=0)), ("sec", "tm", "dp")
    )
    grad_mean = sum_grad / all_count
    cross_mean = sum_cross / all_count
    d_conv = (bn_gain * bn_rstd * (d_pre - grad_mean - z_hat * cross_mean)).astype(jnp.bfloat16)
    conv_rows = extended(d_conv, ((("sec", "tm"), 0),), half_width).astype(jnp.float32)
    d_gated = jnp.zeros((frames, feat_width), jnp.float32)
    for tap_idx in range(tap_count):
        lead = 2 * half_width - tap_idx
        d_gated = (
            d_gated
            + dw_kernel[tap_idx]
            * agree_mask(segment, inside, 2 * half_width, frames, half_width - tap_idx)
            * conv_rows[lead : lead + frames]
        )
    d_mixed = jnp.concatenate(
        [d_gated * gate_sig, d_gated * lin_part * gate_sig * (1.0 - gate_sig)], axis=1
    ).astype(jnp.bfloat16)
    d_normed = dot_transposed(d_mixed, w_in)
    h_term = d_normed * ln_gain
    back_norm = row_rstd * (
        h_term
        - jnp.mean(h_term, axis=1, keepdims=True)
        - x_hat * jnp.mean(h_term * x_hat, axis=1, keepdims=True)
    )
    grad_input = (incoming.astype(jnp.float32) + back_norm).astype(jnp.bfloat16)
    return grad_input[None]


def solution(mesh):
    in_specs = (
        P("dp", ("sec", "tm"), None),
        P("dp", ("sec", "tm"), None),
        P("dp", ("sec", "tm")),
        P("dp", None),
        P(),
        P(),
        P(),
        P(),
        P(),
        P(),
        P(),
    )
    out_specs = P("dp", ("sec", "tm"), None)
    return jax.shard_map(local, mesh=mesh, in_specs=in_specs, out_specs=out_specs, check_vma=False)
```

profile of v0, /device:TPU:1, one launch (start us, length us, event | category | flops | bytes accessed | tf_op | source)
XLA Modules:
  0.0 299.8 jit_solution(17443736165663696732)
XLA Ops:
  0.0 0.0 copy-start
  0.0 0.8 compare_bitcast_fusion
  0.8 0.7 compare_select_fusion
  1.5 0.7 add_bitcast_fusion.2
  2.1 0.2 convert_reduce_fusion.2
  2.3 0.1 select_reduce_fusion
  2.5 0.7 copy.16
  3.2 13.3 %all-to-all-start = ((s32[64,1,1]{2,1,0:T(1,128)}), s32[64,1,1]{2,1,0:T(1,128)S(1)}, u32[]{:S(2)}, u32[]{:S(2)}) async-start(s32[64,1,1]{2,1,0:T(1,128)} %copy.16), calls=%async_computation | async-start | bytes 65536 | tf_op jit(solution)/shard_map/all_to_all | solution.py:86
  16.4 1.4 convert_reduce_fusion
  17.9 1.6 fusion.14
  19.5 4.2 %reshape_squeeze.3 = bf16[64,16384]{1,0:T(8,128)(2,1)} reshape(bf16[1,1024,1024]{2,1,0:T(8,128)(2,1)} %param.12) | data formatting | bytes 4194304 | tf_op jit(solution)/shard_map/reshape;squeeze | solution.py:73
  23.8 3.6 %fusion = bf16[64,1,16384]{2,0,1:T(8,128)(2,1)} fusion(bf16[64,16384]{1,0:T(8,128)(2,1)} %reshape_squeeze.3, s32[64]{0:T(128)S(1)} %get-tuple-element.44, pred[64]{0:T(512)(128)(4,1)S(1)} %compare_bitcast_fusion, pred[64]{0:T(512)(128)(4,1)S(1)} %broadcast_compare_fusion), kind=kOutput, calls=%fused_computation.1 | convolution fusion | flops 135278592 | bytes 4194688 | tf_op jit(solution)/shard_map/dot_general | solution.py:74
  27.4 0.5 broadcast.226
  27.9 4.5 %reduce.6 = bf16[64,16384]{1,0:T(8,128)(2,1)} reduce(bf16[64,1,16384]{2,0,1:T(8,128)(2,1)} %fusion, bf16[]{:T(256)} %broadcast.226), dimensions={1}, to_apply=%copy.17.reduce_sub_computation | reduce | bytes 4194306 | tf_op jit(solution)/shard_map/reshape | solution.py:80
  32.4 4.5 %reshape.132 = bf16[64,2,8192]{2,1,0:T(2,128)(2,1)} reshape(bf16[64,16384]{1,0:T(8,128)(2,1)} %reduce.6) | data formatting | bytes 4194304
  36.9 0.0 all-to-all-done
  36.9 10.5 %all-to-all-start.1 = ((bf16[64,2,8192]{2,1,0:T(2,128)(2,1)}), bf16[64,2,8192]{2,1,0:T(2,128)(2,1)}, u32[]{:S(2)}, u32[]{:S(2)}) async-start(bf16[64,2,8192]{2,1,0:T(2,128)(2,1)} %reshape.132), calls=%async_computation.1 | async-start | bytes 4194304 | tf_op jit(solution)/shard_map/all_to_all | solution.py:79
  47.4 0.0 copy-done.3
  47.4 0.0 copy-done.8
  47.4 0.0 copy-done.11
  47.4 4.6 %fusion.41 = f32[512,2048]{1,0:T(8,128)S(1)} fusion(bf16[1024,2048]{1,0:T(8,128)(2,1)} %param.17, bf16[1,512,1024]{2,1,0:T(8,128)(2,1)S(1)} %copy-done.3, f32[1024]{0:T(1024)S(1)} %copy-done.11, f32[1024]{0:T(1024)S(1)} %copy-done.8, f32[512]{0:T(512)S(1)} %add_rsqrt_fusion.1, f32[512]{0:T(512)S(1)} %broadcast_multiply_fusion.5), kind=kOutput, calls=%fused_computation.75 | convolution fusion | flops 2150629376 | bytes 9449472 | tf_op jit(solution)/shard_map/dot_general | solution.py:111
  52.1 0.0 copy-start.1
  52.1 0.0 copy-start.9
  52.1 0.0 copy-start.6
  52.1 0.6 multiply_convert_fusion.3
  52.7 1.3 copy-done.1
  54.0 1.0 copy-done.4
  55.0 3.3 %collective-permute-start = (bf16[4,1024]{1,0:T(4,128)(2,1)S(1)}, bf16[4,1024]{1,0:T(4,128)(2,1)S(1)}, u32[]{:S(2)}, u32[]{:S(2)}) collective-permute-start(bf16[4,1024]{1,0:T(4,128)(2,1)S(1)} %get-tuple-element.20), channel_id=1, source_target_pairs={{0,4},{4,8},{8,12},{12,16},{16,20},{20,24},{24,28},{28,32},{32,36}... | collective-permute-start | bytes 24584 | tf_op jit(solution)/shard_map/ppermute | solution.py:17
  58.2 5.6 %collective-permute-start.1 = (bf16[4,1024]{1,0:T(4,128)(2,1)S(1)}, bf16[4,1024]{1,0:T(4,128)(2,1)S(1)}, u32[]{:S(2)}, u32[]{:S(2)}) collective-permute-start(bf16[4,1024]{1,0:T(4,128)(2,1)S(1)} %get-tuple-element.21), channel_id=1, source_target_pairs={{4,0},{8,4},{12,8},{16,12},{20,16},{24,20},{28,24},{32,28},{36,32}... | collective-permute-start | bytes 24584 | tf_op jit(solution)/shard_map/ppermute | solution.py:20
  63.9 0.0 copy-done.9
  63.9 0.3 reduce-window.9
  64.2 0.1 slice.229
  64.3 0.1 slice_reduce_fusion
  64.5 0.1 add_bitcast_fusion
  64.5 0.1 convert_reduce_fusion.1
  64.7 0.1 fusion.61
  64.8 0.1 fusion.59
  64.9 0.0 copy-done.6
  64.9 1.2 subtract_reduce_fusion
  66.1 31.5 %collective-permute-done = bf16[4,1024]{1,0:T(4,128)(2,1)S(1)} collective-permute-done((bf16[4,1024]{1,0:T(4,128)(2,1)S(1)}, bf16[4,1024]{1,0:T(4,128)(2,1)S(1)}, u32[]{:S(2)}, u32[]{:S(2)}) %collective-permute-start) | collective-permute-done | bytes 8224 | tf_op jit(solution)/shard_map/ppermute | solution.py:17
  97.7 0.0 collective-permute-done.1
  97.7 1.5 maximum_convert_fusion
  99.2 0.0 copy-start.7
  99.2 4.8 %fusion.75 = (f32[1024]{0:T(1024)S(1)}, f32[1024]{0:T(1024)S(1)}, f32[512,1024]{1,0:T(8,128)}) fusion(f32[520,1024]{1,0:T(8,128)S(1)} %maximum_convert_fusion, f32[512]{0:T(512)S(1)} %get-tuple-element.39, f32[1024]{0:T(1024)S(1)} %bitcast.89, f32[512]{0:T(512)S(1)} %get-tuple-element.40, f32[1024]{0:T(1024)S(1)} %bitcast.91, f32[512]{0:T(512)S(1)} %get-tuple-element.34, ...), kind=kLoop, calls=%fused_computation.151 | loop fusion | flops 15202304 | bytes 21035008 | tf_op jit(solution)/shard_map/reduce_sum | solution.py:132
  104.0 74.8 %all-reduce.2 = (f32[1024]{0:T(1024)S(1)}, f32[1024]{0:T(1024)S(1)}) all-reduce(f32[1024]{0:T(1024)S(1)} %get-tuple-element.10, f32[1024]{0:T(1024)S(1)} %get-tuple-element.9), channel_id=1, replica_groups=mesh['sec'=2,'tm'=32,'dp'=4] {'sec','tm','dp'}, use_global_device_ids=true, to_apply=%region_8.9 | all-reduce | flops 2048 | bytes 16384 | tf_op jit(solution)/shard_map/psum | solution.py:131
  178.8 0.0 all-to-all-done.1
  178.8 10.5 %reshape.133 = bf16[64,1,16384]{2,1,0:T(2,128)(2,1)} reshape(bf16[64,2,8192]{2,1,0:T(2,128)(2,1)} %all-to-all-done.1) | data formatting | bytes 4194304
  189.2 5.7 %convolution_convert_fusion.1 = bf16[32,16384]{1,0:T(8,128)(2,1)} fusion(bf16[64,1,16384]{2,1,0:T(2,128)(2,1)} %reshape.133, s32[64]{0:T(128)S(1)} %subtract_reduce_fusion), kind=kOutput, calls=%fused_computation.2 | convolution fusion | flops 67635200 | bytes 3145984 | tf_op jit(solution)/shard_map/dot_general | solution.py:97
  195.0 2.4 reshape.126
  197.3 0.0 copy-done
  197.3 5.3 %fusion.74 = (f32[1024]{0:T(1024)S(1)}, f32[1024]{0:T(1024)S(1)}, f32[512,1024]{1,0:T(8,128)}) fusion(f32[1024]{0:T(1024)S(1)} %get-tuple-element.32, f32[512,1024]{1,0:T(8,128)} %get-tuple-element.17, f32[1024]{0:T(1024)S(1)} %get-tuple-element.41, f32[1024]{0:T(1024)S(1)} %copy-done.12, f32[1024]{0:T(1024)S(1)} %copy-done.7, ...), kind=kOutput, calls=%fused_computation.150 | convolution fusion | flops 1081604096 | bytes 7364608 | tf_op jit(solution)/shard_map/dot_general | solution.py:33
  202.6 73.6 %all-reduce.1 = (f32[1024]{0:T(1024)S(1)}, f32[1024]{0:T(1024)S(1)}) all-reduce(f32[1024]{0:T(1024)S(1)} %get-tuple-element.8, f32[1024]{0:T(1024)S(1)} %get-tuple-element.7), channel_id=1, replica_groups=mesh['sec'=2,'tm'=32,'dp'=4] {'sec','tm','dp'}, use_global_device_ids=true, to_apply=%region_14.15 | all-reduce | flops 2048 | bytes 16384 | tf_op jit(solution)/shard_map/psum | solution.py:142
  276.3 2.9 multiply_convert_fusion.2
  279.2 2.6 collective-permute-start.2
  281.8 6.5 %collective-permute-start.3 = (bf16[4,1024]{1,0:T(4,128)(2,1)S(1)}, bf16[4,1024]{1,0:T(4,128)(2,1)S(1)}, u32[]{:S(2)}, u32[]{:S(2)}) collective-permute-start(bf16[4,1024]{1,0:T(4,128)(2,1)S(1)} %get-tuple-element.19), channel_id=1, source_target_pairs={{4,0},{8,4},{12,8},{16,12},{20,16},{24,20},{28,24},{32,28},{36,32}... | collective-permute-start | bytes 24584 | tf_op jit(solution)/shard_map/ppermute | solution.py:20
  288.3 0.0 collective-permute-done.2
  288.4 0.5 collective-permute-done.3
  288.9 0.3 maximum_convert_fusion.1
  289.2 3.9 %multiply_convert_fusion.1 = (bf16[512,1024]{1,0:T(8,128)(2,1)S(1)}, f32[512,1024]{1,0:T(8,128)S(1)}) fusion(f32[512,2048]{1,0:T(8,128)S(1)} %copy-done.2, f32[520,1024]{1,0:T(8,128)S(1)} %maximum_convert_fusion.1, f32[512]{0:T(512)S(1)} %get-tuple-element.33, f32[1024]{0:T(1024)S(1)} %bitcast.90, f32[512]{0:T(512)S(1)} %get-tuple-element.37, ...), kind=kLoop, calls=%fused_computation.64 | loop fusion | flops 16252928 | bytes 24172544 | tf_op jit(solution)/shard_map/convert
  293.1 0.0 copy-start.10
  293.1 0.9 multiply_convert_fusion
  294.0 1.3 copy-done.10
  295.3 2.6 multiply_reduce_fusion.2
  297.9 1.8 fusion.40
  (27 shorter events, 0.2 us)
Async XLA Ops:
  0.0 197.3 %copy-start = (bf16[1024,1024]{1,0:T(8,128)(2,1)S(1)}, bf16[1024,1024]{1,0:T(8,128)(2,1)}, u32[]{:S(2)}) copy-start(bf16[1024,1024]{1,0:T(8,128)(2,1)} %param.21) | copy-start | bytes 6291460
  3.2 33.7 %all-to-all-start = ((s32[64,1,1]{2,1,0:T(1,128)}), s32[64,1,1]{2,1,0:T(1,128)S(1)}, u32[]{:S(2)}, u32[]{:S(2)}) async-start(s32[64,1,1]{2,1,0:T(1,128)} %copy.16), calls=%async_computation | async-start | bytes 65536 | tf_op jit(solution)/shard_map/all_to_all | solution.py:86
  36.9 10.5 %copy-start.3 = (bf16[1,512,1024]{2,1,0:T(8,128)(2,1)S(1)}, bf16[1,512,1024]{2,1,0:T(8,128)(2,1)}, u32[]{:S(2)}) copy-start(bf16[1,512,1024]{2,1,0:T(8,128)(2,1)} %param.11) | copy-start | bytes 3145732
  36.9 10.5 %copy-start.8 = (f32[1024]{0:T(1024)S(1)}, f32[1024]{0:T(1024)}, u32[]{:S(2)}) copy-start(f32[1024]{0:T(1024)} %param.15) | copy-start | bytes 12292
  36.9 10.6 %copy-start.11 = (f32[1024]{0:T(1024)S(1)}, f32[1024]{0:T(1024)}, u32[]{:S(2)}) copy-start(f32[1024]{0:T(1024)} %param.16) | copy-start | bytes 12292
  36.9 141.9 %all-to-all-start.1 = ((bf16[64,2,8192]{2,1,0:T(2,128)(2,1)}), bf16[64,2,8192]{2,1,0:T(2,128)(2,1)}, u32[]{:S(2)}, u32[]{:S(2)}) async-start(bf16[64,2,8192]{2,1,0:T(2,128)(2,1)} %reshape.132), calls=%async_computation.1 | async-start | bytes 4194304 | tf_op jit(solution)/shard_map/all_to_all | solution.py:79
  52.1 1.9 copy-start.1
  52.1 11.8 %copy-start.9 = (s32[1,262]{1,0:T(1,128)S(1)}, s32[1,262]{1,0:T(1,128)}, u32[]{:S(2)}) copy-start(s32[1,262]{1,0:T(1,128)} %param.14) | copy-start | bytes 3148
  52.1 12.8 %copy-start.6 = (f32[9,1024]{1,0:T(8,128)S(1)}, f32[9,1024]{1,0:T(8,128)}, u32[]{:S(2)}) copy-start(f32[9,1024]{1,0:T(8,128)} %param.18) | copy-start | bytes 110596
  54.0 1.0 copy-start.4
  55.0 42.7 %collective-permute-start = (bf16[4,1024]{1,0:T(4,128)(2,1)S(1)}, bf16[4,1024]{1,0:T(4,128)(2,1)S(1)}, u32[]{:S(2)}, u32[]{:S(2)}) collective-permute-start(bf16[4,1024]{1,0:T(4,128)(2,1)S(1)} %get-tuple-element.20), channel_id=1, source_target_pairs={{0,4},{4,8},{8,12},{12,16},{16,20},{20,24},{24,28},{28,32},{32,36}... | collective-permute-start | bytes 24584 | tf_op jit(solution)/shard_map/ppermute | solution.py:17
  58.2 39.4 %collective-permute-start.1 = (bf16[4,1024]{1,0:T(4,128)(2,1)S(1)}, bf16[4,1024]{1,0:T(4,128)(2,1)S(1)}, u32[]{:S(2)}, u32[]{:S(2)}) collective-permute-start(bf16[4,1024]{1,0:T(4,128)(2,1)S(1)} %get-tuple-element.21), channel_id=1, source_target_pairs={{4,0},{8,4},{12,8},{16,12},{20,16},{24,20},{28,24},{32,28},{36,32}... | collective-permute-start | bytes 24584 | tf_op jit(solution)/shard_map/ppermute | solution.py:20
  99.2 79.6 %copy-start.7 = (f32[1024]{0:T(1024)S(1)}, f32[1024]{0:T(1024)}, u32[]{:S(2)}) copy-start(f32[1024]{0:T(1024)} %param.19) | copy-start | bytes 12292
  189.2 8.1 %copy-start.12 = (f32[1024]{0:T(1024)S(1)}, f32[1024]{0:T(1024)}, u32[]{:S(2)}) copy-start(f32[1024]{0:T(1024)} %param.20) | copy-start | bytes 12292
  276.3 12.9 %copy-start.2 = (f32[512,2048]{1,0:T(8,128)S(1)}, f32[512,2048]{1,0:T(8,128)}, u32[]{:S(2)}) copy-start(f32[512,2048]{1,0:T(8,128)} %copy-done.1) | copy-start | bytes 12582916
  279.2 9.1 %collective-permute-start.2 = (bf16[4,1024]{1,0:T(4,128)(2,1)S(1)}, bf16[4,1024]{1,0:T(4,128)(2,1)S(1)}, u32[]{:S(2)}, u32[]{:S(2)}) collective-permute-start(bf16[4,1024]{1,0:T(4,128)(2,1)S(1)} %get-tuple-element.18), channel_id=1, source_target_pairs={{0,4},{4,8},{8,12},{12,16},{16,20},{20,24},{24,28},{28,32},{32,36}... | collective-permute-start | bytes 24584 | tf_op jit(solution)/shard_map/ppermute | solution.py:17
  281.8 7.1 %collective-permute-start.3 = (bf16[4,1024]{1,0:T(4,128)(2,1)S(1)}, bf16[4,1024]{1,0:T(4,128)(2,1)S(1)}, u32[]{:S(2)}, u32[]{:S(2)}) collective-permute-start(bf16[4,1024]{1,0:T(4,128)(2,1)S(1)} %get-tuple-element.19), channel_id=1, source_target_pairs={{4,0},{8,4},{12,8},{16,12},{20,16},{24,20},{28,24},{32,28},{36,32}... | collective-permute-start | bytes 24584 | tf_op jit(solution)/shard_map/ppermute | solution.py:20
  293.1 2.2 copy-start.10
  295.3 2.6 copy-start.5
where the time goes:
time: 301 us; the launch traced here: 300 us
  blocking collectives  148 us (49%)
  starting transfers between devices  41.7 us (14%)
  waiting for transfers between devices  32.1 us (11%)
  other arithmetic  28.7 us (10%)
  local copies, waits for them, and re-layouts  26.6 us (9%)
  matrix products  21.9 us (7%)
    psum x1, blocking collectives, local(): lax.psum((jnp.sum(conv_out, axis=0), jnp.sum(conv_out * conv_out, axis=0)...  74.8 us
    psum x1, blocking collectives, local(): lax.psum((jnp.sum(d_pre, axis=0), jnp.sum(d_pre * z_hat, axis=0)), ('sec'...  73.6 us
    ppermute x2, waiting for transfers between devices, extended(): lax.ppermute(lax.slice_in_dim(block, block.shape[dim] - width, None, axis...  31.5 us
    unnamed x28, local copies, waits for them, and re-layouts  18.6 us
    all_to_all x1, starting transfers between devices, local(): lax.all_to_all(packed_ids.reshape(shards, capacity), ('sec', 'tm'), split...  13.3 us
    ppermute x2, starting transfers between devices, extended(): lax.ppermute(lax.slice_in_dim(block, 0, width, axis=dim), axis, backward)  12.1 us
    all_to_all x1, starting transfers between devices, local(): lax.all_to_all(packed.reshape(shards, capacity, block_rows * feat_width),...  10.5 us
    dot_general x2, matrix products, dot_transposed(): lax.dot_general(left_side, weight, (((1,), (1,)), ((), ())), preferred_el...  7.9 us
  transfers between devices with their start and end apart: 6, of which 2 were waited for; matrix products, arithmetic and copies ran while one was open for 11% of the time, Pallas kernels for 0%

commit v1 on v0

v1 whole, which is shorter than its diff:
```python
import functools

import jax
import jax.numpy as jnp
from jax import lax
from jax.experimental import pallas as pl
from jax.experimental.pallas import tpu as pltpu
from jax.sharding import PartitionSpec as P

MESH = pl.DeviceIdType.MESH
F32 = jnp.float32
BF16 = jnp.bfloat16
I32 = jnp.int32

EPS = 1e-05
SEC, NZ, NY, NX = 2, 8, 4, 4
SHARDS = SEC * NZ * NY
FRAMES = 512
C = 1024
TAPS = 9
HALF = 4
PAD = 8
EXT = FRAMES + 2 * PAD
BLK = 16
NBE = 32
UTT = 262
UTT_PAD = 384
LANES = 128
COLS = C // LANES
ROWS = 128
WIN = 6
SENDS = SHARDS - 1
ALL_FRAMES = float(FRAMES * SHARDS * NX)
NT = (((1,), (1,)), ((), ()))


def wrap(value, count):
    return lax.rem(value + count, count)


def kernel(
    enc_hbm,
    llm_hbm,
    w_in_hbm,
    w_out_hbm,
    slot_ref,
    utt_ref,
    ln_gain_ref,
    ln_bias_ref,
    dw_ref,
    bn_gain_ref,
    bn_bias_ref,
    out_hbm,
    enc,
    llm,
    w_in,
    w_out,
    send,
    recv,
    row_buf,
    slot_tbl,
    src_tbl,
    ids_line,
    ids_tile,
    ids_all,
    utt_pad,
    seg,
    masks,
    x_hat,
    rstd,
    normed,
    sig,
    dsig,
    gated,
    conv,
    swish,
    ones_t,
    z_t,
    d_t,
    d_pre,
    inc,
    d_mixed,
    h_buf,
    out_buf,
    ar_src,
    ar_s,
    ar_xy,
    ar_z,
    load_sem,
    tbl_sem,
    a2a_send,
    a2a_recv,
    ids_send,
    ids_recv,
    halo_send,
    halo_recv,
    ar_send,
    ar_recv,
    out_sem,
):
    sec = lax.axis_index("sec")
    tm = lax.axis_index("tm")
    dp = lax.axis_index("dp")
    z = tm // NY
    y = lax.rem(tm, NY)
    me = sec * (NZ * NY) + tm

    def place(s_at, z_at, y_at, x_at):
        return {"sec": s_at, "tm": z_at * NY + y_at, "dp": x_at}

    loads = []
    for k, (source, target) in enumerate(
        ((llm_hbm, llm), (enc_hbm, enc), (w_in_hbm, w_in), (w_out_hbm, w_out))
    ):
        load = pltpu.make_async_copy(source, target, load_sem.at[k])
        load.start()
        loads.append(load)

    def partner(i):
        k = lax.rem(i, NZ)
        q = 7 - i // NZ
        dz = 4 + ((k + 1) // 2) * (1 - 2 * lax.rem(k, 2))
        return (
            lax.rem(sec + lax.rem(q, 2), SEC),
            lax.rem(z + dz, NZ),
            lax.rem(y + q // 2, NY),
        )

    line = [(sec, wrap(z + d, NZ), y, dp) for d in (4, 3, 5, 2, 6, 1, 7)]
    cross = [
        (sec, z, wrap(y + j, NY), wrap(dp + i, NX))
        for j in (2, 1, 3, 0)
        for i in (2, 1, 3, 0)
        if (i, j) != (0, 0)
    ]
    mate = [(1 - sec, z, y, dp)]
    plane = [
        (wrap(sec + s, SEC), z, wrap(y + j, NY), dp)
        for j in (2, 1, 3, 0)
        for s in (1, 0)
        if (s, j) != (0, 0)
    ]

    barrier = pltpu.get_barrier_semaphore()

    def greet(i, carry):
        s_at, z_at, y_at = partner(i)
        pl.semaphore_signal(
            barrier, inc=1, device_id=place(s_at, z_at, y_at, dp), device_id_type=MESH
        )
        return carry

    lax.fori_loop(0, SENDS, greet, 0)
    others = [p for p, keep in zip(cross, [i != 0 for j in (2, 1, 3, 0) for i in (2, 1, 3, 0) if (i, j) != (0, 0)]) if keep]
    for p in others:
        pl.semaphore_signal(barrier, inc=1, device_id=place(*p), device_id_type=MESH)

    slot_row = slot_ref[...]
    lane = lax.broadcasted_iota(I32, (64, LANES), 1)
    sub = lax.broadcasted_iota(I32, (64, LANES), 0)
    lane64 = lax.broadcasted_iota(I32, (64, 64), 1)
    sub64 = lax.broadcasted_iota(I32, (64, 64), 0)
    slot_col = jnp.sum(
        jnp.where(lane64 == sub64, jnp.broadcast_to(slot_row, (64, 64)), 0), axis=1, keepdims=True
    )
    hit = (slot_col >= lane * NBE) & (slot_col < lane * NBE + NBE)
    row_buf[0:1, :] = jnp.sum(jnp.where(hit, sub, 0), axis=0, keepdims=True)
    ids_row = jnp.sum(jnp.where(hit, slot_col + 1, 0), axis=0, keepdims=True) - 1
    tbl = pltpu.make_async_copy(row_buf.at[pl.ds(0, 1)], slot_tbl, tbl_sem.at[0])
    tbl.start()
    ids_line[z] = ids_row
    loads[0].wait()
    tbl.wait()

    def pack(d, carry):
        send[d] = llm[jnp.clip(slot_tbl[0, d], 0, 63)]
        return carry

    lax.fori_loop(0, SHARDS, pack, 0)
    recv[me] = send[me]

    pl.semaphore_wait(barrier, SENDS + len(others))

    def spread(partners, source, target_of, s_sem, r_sem):
        for i, p in enumerate(partners):
            pltpu.make_async_remote_copy(
                source, target_of(i), s_sem, r_sem, device_id=place(*p), device_id_type=MESH
            ).start()

    def wait_bytes(ref, sem):
        pltpu.make_async_copy(ref, ref, sem).wait()

    spread(line, ids_line.at[z], lambda i: ids_line.at[z], ids_send.at[0], ids_recv.at[0])

    def block_copy(i):
        s_at, z_at, y_at = partner(i)
        to = s_at * (NZ * NY) + z_at * NY + y_at
        return pltpu.make_async_remote_copy(
            send.at[to],
            recv.at[me],
            a2a_send.at[lax.rem(i, WIN)],
            a2a_recv,
            device_id=place(s_at, z_at, y_at, dp),
            device_id_type=MESH,
        )

    def first(i, carry):
        block_copy(i).start()
        return carry

    lax.fori_loop(0, WIN, first, 0)
    sent = [WIN]

    def pump_one(i):
        block_copy(i - WIN).wait_send()
        block_copy(i).start()

    def pump(count):
        low = sent[0]
        high = min(SENDS, low + count)
        sent[0] = high
        if high > low:

            def step(i, carry):
                pump_one(i)
                return carry

            lax.fori_loop(low, high, step, 0)

    def pumped(count):
        low = sent[0]
        assert low + count <= SENDS
        sent[0] = low + count
        return low

    loads[1].wait()
    gain = ln_gain_ref[...]
    bias = ln_bias_ref[...]

    def norm(r, carry):
        rows = pl.ds(pl.multiple_of(r * 64, 64), 64)
        values = enc[rows, :].astype(F32)
        mean = jnp.mean(values, axis=1, keepdims=True)
        centred = values - mean
        scale = lax.rsqrt(jnp.mean(centred * centred, axis=1, keepdims=True) + EPS)
        hat = centred * scale
        rstd[rows, :] = jnp.broadcast_to(scale, (64, LANES))
        x_hat[rows, :] = hat
        normed[rows, :] = (hat * gain + bias).astype(BF16)
        return carry

    lax.fori_loop(0, 8, norm, 0)
    pump(2)

    loads[2].wait()
    low = pumped(8)

    def project(n, carry):
        at = pl.ds(pl.multiple_of(n * 256, 256), 256)
        gate_at = pl.ds(pl.multiple_of(C + n * 256, 256), 256)
        lin = jnp.dot(normed[...], w_in[:, at], preferred_element_type=F32)
        gate = jnp.dot(normed[...], w_in[:, gate_at], preferred_element_type=F32)
        pump_one(low + 2 * n)
        s = jax.nn.sigmoid(gate)
        mixed = lin * s
        sig[:, at] = s
        dsig[:, at] = mixed * (1.0 - s)
        gated[pl.ds(PAD, FRAMES), at] = mixed.astype(BF16).astype(F32)
        pump_one(low + 2 * n + 1)
        return carry

    lax.fori_loop(0, 4, project, 0)

    before = wrap(me + SHARDS - 1, SHARDS)
    after = wrap(me + 1, SHARDS)

    def edges(buf, k):
        for j, (to, start, end) in enumerate(
            ((after, FRAMES, 0), (before, PAD, PAD + FRAMES))
        ):
            pltpu.make_async_remote_copy(
                buf.at[pl.ds(start, PAD)],
                buf.at[pl.ds(end, PAD)],
                halo_send.at[k, j],
                halo_recv.at[k, j],
                device_id={"sec": to // (NZ * NY), "tm": lax.rem(to, NZ * NY), "dp": dp},
                device_id_type=MESH,
            ).start()

    def edges_in(buf, k):
        wait_bytes(buf.at[pl.ds(0, PAD)], halo_recv.at[k, 0])
        wait_bytes(buf.at[pl.ds(PAD + FRAMES, PAD)], halo_recv.at[k, 1])

    def edges_out(buf, k):
        wait_bytes(buf.at[pl.ds(0, PAD)], halo_send.at[k, 0])
        wait_bytes(buf.at[pl.ds(0, PAD)], halo_send.at[k, 1])

    edges(gated, 0)

    wait_bytes(ids_line.at[pl.ds(0, NZ - 1)], ids_recv.at[0])
    for j in range(NZ):
        ids_tile[j : j + 1, :] = ids_line[j]
    here = sec * NY + y
    ids_all[here] = ids_tile[...]
    spread(plane, ids_tile, lambda i: ids_all.at[here], ids_send.at[1], ids_recv.at[1])

    utt_pad[...] = jnp.zeros((8, UTT_PAD), I32)
    utt_pad[0:1, 0:UTT] = utt_ref[...]
    lengths = utt_pad[...].astype(F32).astype(BF16)
    upper = (
        lax.broadcasted_iota(I32, (UTT_PAD, UTT_PAD), 0)
        <= lax.broadcasted_iota(I32, (UTT_PAD, UTT_PAD), 1)
    ).astype(F32).astype(BF16)
    ends = jnp.dot(lengths, upper, preferred_element_type=F32)[0:1, :]

    def number(r, carry):
        rows = pl.ds(pl.multiple_of(r * 48, 8), 48)
        position = lax.broadcasted_iota(I32, (48, 1), 0) + (r * 48 + me * FRAMES - PAD)
        position_f = position.astype(F32)
        count = jnp.sum((position_f >= ends).astype(F32), axis=1, keepdims=True)
        inside = (position >= 0) & (position < SHARDS * FRAMES)
        seg[rows, :] = jnp.broadcast_to(jnp.where(inside, count, -1.0), (48, LANES))
        return carry

    lax.fori_loop(0, EXT // 48, number, 0)

    def mark(r, carry):
        window = seg[pl.ds(pl.multiple_of(r * ROWS, ROWS), ROWS + 2 * PAD), :]
        own = window[PAD : PAD + ROWS]
        rows = pl.ds(pl.multiple_of(r * ROWS, ROWS), ROWS)
        for j in range(TAPS):
            masks[j, rows, :] = (window[HALF + j : HALF + j + ROWS] == own).astype(F32)
        return carry

    lax.fori_loop(0, FRAMES // ROWS, mark, 0)
    pump(5)
    edges_in(gated, 0)

    low_conv = pumped(8)

    def convolve(c, carry):
        cols = pl.ds(pl.multiple_of(c * LANES, LANES), LANES)
        taps = dw_ref[:, cols]
        first_sum = jnp.zeros((1, LANES), F32)
        second_sum = jnp.zeros((1, LANES), F32)
        for r in range(FRAMES // ROWS):
            window = gated[r * ROWS : r * ROWS + ROWS + 2 * PAD, cols]
            total = jnp.zeros((ROWS, LANES), F32)
            for k in range(TAPS):
                part = window[HALF + k : HALF + k + ROWS]
                if k != HALF:
                    part = part * masks[k, r * ROWS : r * ROWS + ROWS, :]
                total = total + taps[k : k + 1, :] * part
            conv[PAD + r * ROWS : PAD + r * ROWS + ROWS, cols] = total
            first_sum = first_sum + jnp.sum(total, axis=0, keepdims=True)
            second_sum = second_sum + jnp.sum(total * total, axis=0, keepdims=True)
        ar_src[0, 0, 0, pl.ds(c, 1), :] = first_sum
        ar_src[0, 0, 1, pl.ds(c, 1), :] = second_sum
        pump_one(low_conv + c)
        return carry

    lax.fori_loop(0, COLS, convolve, 0)
    edges(conv, 1)

    groups = ((mate, ar_s), (cross, ar_xy), (line, ar_z))

    def sum_send(k, step):
        partners, target = groups[step]
        spread(
            partners,
            ar_src.at[k, step],
            lambda i: target.at[k, i],
            ar_send.at[k, step],
            ar_recv.at[k, step],
        )

    def sum_recv(k, step):
        partners, target = groups[step]
        count = len(partners)
        wait_bytes(target.at[k, pl.ds(0, count)], ar_recv.at[k, step])
        total = ar_src[k, step]
        for i in range(count):
            total = total + target[k, i]
        ar_src[k, step + 1] = total

    def sum_done(k):
        for step, (partners, target) in enumerate(groups):
            wait_bytes(target.at[k, pl.ds(0, len(partners))], ar_send.at[k, step])

    for step, count in ((0, 1), (1, 7), (2, 7)):
        sum_send(0, step)
        pump(count)
        sum_recv(0, step)

    wait_bytes(ids_all.at[pl.ds(0, 7)], ids_recv.at[1])
    ids = ids_all[...].reshape(64, LANES)
    mine = jnp.sum(jnp.where(lane == me, ids, 0), axis=1, keepdims=True) - me * NBE
    quarter = sub // NZ
    source = (quarter // NY) * (NZ * NY) + lax.rem(sub, NZ) * NY + lax.rem(quarter, NY)
    row_buf[1:2, :] = jnp.sum(jnp.where(mine == lane, source, 0), axis=0, keepdims=True)
    src_copy = pltpu.make_async_copy(row_buf.at[pl.ds(1, 1)], src_tbl, tbl_sem.at[1])
    src_copy.start()

    edges_in(conv, 1)
    edges_out(conv, 1)

    low_bn = pumped(8)

    def bn_scales(c):
        bn_mean = ar_src[0, 3, 0, pl.ds(c, 1), :] / ALL_FRAMES
        bn_var = ar_src[0, 3, 1, pl.ds(c, 1), :] / ALL_FRAMES - bn_mean * bn_mean
        return bn_mean, lax.rsqrt(bn_var + EPS)

    def transposed(source, c, r, window_of):
        taps = dw_ref[:, pl.ds(pl.multiple_of(c * LANES, LANES), LANES)]
        return taps

    def normalise(c, carry):
        cols = pl.ds(pl.multiple_of(c * LANES, LANES), LANES)
        bn_mean, bn_rstd = bn_scales(c)
        bn_gain = bn_gain_ref[pl.ds(c, 1), :]
        bn_bias = bn_bias_ref[pl.ds(c, 1), :]
        taps = dw_ref[:, cols]
        factor = bn_gain * bn_rstd
        for r in range(EXT // 48):
            rows = slice(r * 48, r * 48 + 48)
            conv[rows, cols] = (conv[rows, cols] - bn_mean) * bn_rstd
        for r in range(FRAMES // ROWS):
            rows = slice(r * ROWS, r * ROWS + ROWS)
            window = conv[r * ROWS : r * ROWS + ROWS + 2 * PAD, cols]
            pre = window[PAD : PAD + ROWS] * bn_gain + bn_bias
            s = jax.nn.sigmoid(pre)
            swish[rows, cols] = s * (1.0 + pre * (1.0 - s))
            ones_total = jnp.zeros((ROWS, LANES), F32)
            z_total = jnp.zeros((ROWS, LANES), F32)
            for j in range(TAPS):
                weight = (taps[TAPS - 1 - j : TAPS - j, :] * factor) * masks[j, rows, :]
                ones_total = ones_total + weight
                z_total = z_total + weight * window[HALF + j : HALF + j + ROWS]
            ones_t[rows, cols] = ones_total
            z_t[rows, cols] = z_total
        pump_one(low_bn + c)
        return carry

    lax.fori_loop(0, COLS, normalise, 0)
    src_copy.wait()
    loads[3].wait()
    pump(SENDS)

    wait_bytes(recv.at[pl.ds(0, SENDS)], a2a_recv)

    def gather(b, carry):
        inc[pl.ds(pl.multiple_of(b * BLK, BLK), BLK), :] = recv[jnp.clip(src_tbl[0, b], 0, 63)]
        return carry

    lax.fori_loop(0, NBE, gather, 0)

    def back(n, carry):
        at = pl.ds(pl.multiple_of(n * 256, 256), 256)
        grad = lax.dot_general(inc[...], w_out[at, :], NT, preferred_element_type=F32)
        grad = grad * swish[:, at]
        d_pre[pl.ds(PAD, FRAMES), at] = grad
        first_sum = jnp.sum(grad, axis=0, keepdims=True)
        cross_sum = jnp.sum(grad * conv[pl.ds(PAD, FRAMES), at], axis=0, keepdims=True)
        for j in range(2):
            ar_src[1, 0, 0, pl.ds(2 * n + j, 1), :] = first_sum[:, j * LANES : (j + 1) * LANES]
            ar_src[1, 0, 1, pl.ds(2 * n + j, 1), :] = cross_sum[:, j * LANES : (j + 1) * LANES]
        return carry

    lax.fori_loop(0, 4, back, 0)

    def conv_back(c, carry):
        cols = pl.ds(pl.multiple_of(c * LANES, LANES), LANES)
        bn_mean, bn_rstd = bn_scales(c)
        factor = bn_gain_ref[pl.ds(c, 1), :] * bn_rstd
        taps = dw_ref[:, cols] * factor
        for r in range(FRAMES // ROWS):
            rows = slice(r * ROWS, r * ROWS + ROWS)
            window = d_pre[r * ROWS : r * ROWS + ROWS + 2 * PAD, cols]
            total = jnp.zeros((ROWS, LANES), F32)
            for j in range(TAPS):
                part = window[HALF + j : HALF + j + ROWS]
                if j != HALF:
                    part = part * masks[j, rows, :]
                total = total + taps[TAPS - 1 - j : TAPS - j, :] * part
            d_t[rows, cols] = total
        return carry

    sum_send(1, 0)
    edges(d_pre, 2)
    sum_recv(1, 0)
    sum_send(1, 1)
    edges_in(d_pre, 2)
    lax.fori_loop(0, COLS // 2, conv_back, 0)
    sum_recv(1, 1)
    sum_send(1, 2)
    lax.fori_loop(COLS // 2, COLS, conv_back, 0)
    sum_recv(1, 2)

    def assemble(c, carry):
        cols = pl.ds(pl.multiple_of(c * LANES, LANES), LANES)
        gate_cols = pl.ds(pl.multiple_of(C + c * LANES, LANES), LANES)
        grad_mean = ar_src[1, 3, 0, pl.ds(c, 1), :] / ALL_FRAMES
        cross_mean = ar_src[1, 3, 1, pl.ds(c, 1), :] / ALL_FRAMES
        for r in range(FRAMES // ROWS):
            rows = slice(r * ROWS, r * ROWS + ROWS)
            grad = d_t[rows, cols] - grad_mean * ones_t[rows, cols] - cross_mean * z_t[rows, cols]
            d_mixed[rows, cols] = (grad * sig[rows, cols]).astype(BF16)
            d_mixed[rows, gate_cols] = (grad * dsig[rows, cols]).astype(BF16)
        return carry

    lax.fori_loop(0, COLS, assemble, 0)

    def unproject(n, carry):
        at = pl.ds(pl.multiple_of(n * 256, 256), 256)
        grad = lax.dot_general(d_mixed[...], w_in[at, :], NT, preferred_element_type=F32)
        h_buf[:, at] = grad * ln_gain_ref[:, at]
        return carry

    lax.fori_loop(0, 4, unproject, 0)

    stores = []
    for r in range(4):
        rows = pl.ds(r * ROWS, ROWS)

        def finish(k, carry, r=r):
            part = pl.ds(pl.multiple_of(r * ROWS + k * 32, 32), 32)
            h = h_buf[part, :]
            hat = x_hat[part, :]
            mean = jnp.mean(h, axis=1, keepdims=True)
            along = jnp.mean(h * hat, axis=1, keepdims=True)
            scale = rstd[part, 0:1]
            out_buf[part, :] = (inc[part, :].astype(F32) + scale * (h - mean - hat * along)).astype(BF16)
            return carry

        lax.fori_loop(0, 4, finish, 0)
        store = pltpu.make_async_copy(out_buf.at[rows], out_hbm.at[rows], out_sem.at[r])
        store.start()
        stores.append(store)

    def drain(i, carry):
        block_copy(i).wait_send()
        return carry

    lax.fori_loop(SENDS - WIN, SENDS, drain, 0)
    wait_bytes(ids_line.at[pl.ds(0, NZ - 1)], ids_send.at[0])
    wait_bytes(ids_all.at[pl.ds(0, 7)], ids_send.at[1])
    edges_out(gated, 0)
    edges_out(d_pre, 2)
    sum_done(0)
    sum_done(1)
    for store in stores:
        store.wait()


def local(
    enc_input,
    llm_grads,
    slot_block,
    utt_lengths,
    ln_gain,
    ln_bias,
    w_in,
    dw_kernel,
    bn_gain,
    bn_bias,
    w_out,
):
    vmem = pl.BlockSpec(memory_space=pltpu.VMEM)
    hbm = pl.BlockSpec(memory_space=pl.ANY)
    dma = pltpu.SemaphoreType.DMA
    full = pltpu.VMEM((FRAMES, C), F32)
    wide = pltpu.VMEM((EXT, C), F32)
    blocks = pltpu.VMEM((SHARDS, BLK, C), BF16)
    out = pl.pallas_call(
        kernel,
        out_shape=jax.ShapeDtypeStruct((FRAMES, C), BF16),
        in_specs=[hbm] * 4 + [vmem] * 7,
        out_specs=hbm,
        scratch_shapes=[
            pltpu.VMEM((FRAMES, C), BF16),
            blocks,
            pltpu.VMEM((C, 2 * C), BF16),
            pltpu.VMEM((C, C), BF16),
            blocks,
            blocks,
            pltpu.VMEM((8, LANES), I32),
            pltpu.SMEM((1, LANES), I32),
            pltpu.SMEM((1, LANES), I32),
            pltpu.VMEM((NZ, 1, LANES), I32),
            pltpu.VMEM((NZ, LANES), I32),
            pltpu.VMEM((8, NZ, LANES), I32),
            pltpu.VMEM((8, UTT_PAD), I32),
            pltpu.VMEM((EXT, LANES), F32),
            pltpu.VMEM((TAPS, FRAMES, LANES), F32),
            full,
            pltpu.VMEM((FRAMES, LANES), F32),
            pltpu.VMEM((FRAMES, C), BF16),
            full,
            full,
            wide,
            wide,
            full,
            full,
            full,
            full,
            wide,
            pltpu.VMEM((FRAMES, C), BF16),
            pltpu.VMEM((FRAMES, 2 * C), BF16),
            full,
            pltpu.VMEM((FRAMES, C), BF16),
            pltpu.VMEM((2, 4, 2, COLS, LANES), F32),
            pltpu.VMEM((2, 1, 2, COLS, LANES), F32),
            pltpu.VMEM((2, 15, 2, COLS, LANES), F32),
            pltpu.VMEM((2, 7, 2, COLS, LANES), F32),
            dma((4,)),
            dma((2,)),
            dma((WIN,)),
            dma,
            dma((2,)),
            dma((2,)),
            dma((3, 2)),
            dma((3, 2)),
            dma((2, 3)),
            dma((2, 3)),
            dma((4,)),
        ],
        compiler_params=pltpu.CompilerParams(
            collective_id=1, has_side_effects=True, vmem_limit_bytes=56 << 20
        ),
        name="conv_module_back",
    )(
        enc_input[0],
        llm_grads[0].reshape(SHARDS, BLK, C),
        w_in,
        w_out,
        slot_block,
        utt_lengths,
        ln_gain.reshape(1, C),
        ln_bias.reshape(1, C),
        dw_kernel,
        bn_gain.reshape(COLS, LANES),
        bn_bias.reshape(COLS, LANES),
    )
    return out[None]


def solution(mesh):
    in_specs = (
        P("dp", ("sec", "tm"), None),
        P("dp", ("sec", "tm"), None),
        P("dp", ("sec", "tm")),
        P("dp", None),
        P(),
        P(),
        P(),
        P(),
        P(),
        P(),
        P(),
    )
    out_specs = P("dp", ("sec", "tm"), None)
    return jax.shard_map(local, mesh=mesh, in_specs=in_specs, out_specs=out_specs, check_vma=False)
```

time: 301 us -> 92.7 us (0.31)
  blocking collectives: 148 us -> 0 us
  Pallas kernels: 0 us -> 90.3 us
  starting transfers between devices: 41.7 us -> 0 us
  waiting for transfers between devices: 32.1 us -> 0 us
  other arithmetic: 28.7 us -> 0 us
  local copies, waits for them, and re-layouts: 26.6 us -> 2.26 us
  matrix products: 21.9 us -> 0 us
    psum x2 -> x0, blocking collectives: 148 us -> none  [the longest x1 74.8 us: local(): lax.psum((jnp.sum(conv_out, axis=0), jnp.sum(conv_out * conv_out, axis=0)...]
    pallas_call x0 -> x1, Pallas kernels: none -> 90.3 us  [local(): pl.pallas_call(kernel, out_shape=jax.ShapeDtypeStruct((FRAMES, C), BF16),...]
    ppermute x4 -> x0, waiting for transfers between devices: 32.1 us -> none  [the longest x2 31.5 us: extended(): lax.ppermute(lax.slice_in_dim(block, block.shape[dim] - width, None, axis...]
    all_to_all x2 -> x0, starting transfers between devices: 23.8 us -> none  [the longest x1 13.3 us: local(): lax.all_to_all(packed_ids.reshape(shards, capacity), ('sec', 'tm'), split...]
    dot_general x5 -> x0, matrix products: 21.9 us -> none  [the longest x2 7.9 us: dot_transposed(): lax.dot_general(left_side, weight, (((1,), (1,)), ((), ())), preferred_el...]
    ppermute x4 -> x0, starting transfers between devices: 18 us -> none  [the longest x2 12.1 us: extended(): lax.ppermute(lax.slice_in_dim(block, 0, width, axis=dim), axis, backward)]
    unnamed x28 -> x1, local copies, waits for them, and re-layouts: 18.6 us -> 2.26 us
    reduce_sum x6 -> x0, other arithmetic: 8.28 us -> none  [the longest x1 4.77 us: local(): jnp.sum(conv_out, axis=0)]
  transfers between devices with their start and end apart: 6 -> 0, of which waited for: 2 -> 0; matrix products, arithmetic and copies ran while one was open for 11% -> 0% of each run, Pallas kernels for 0% -> 0%
where the time goes in v1:
time: 92.7 us; the launch traced here: 92.6 us
  Pallas kernels  90.3 us (97%)
  local copies, waits for them, and re-layouts  2.26 us (2%)
    pallas_call x1, Pallas kernels, local(): pl.pallas_call(kernel, out_shape=jax.ShapeDtypeStruct((FRAMES, C), BF16),...  90.3 us
    unnamed x1, local copies, waits for them, and re-layouts  2.26 us

profile of v1, /device:TPU:1, one launch (start us, length us, event | category | flops | bytes accessed | tf_op | source)
XLA Modules:
  0.0 92.6 jit_solution(5393329542664100598)
XLA Ops:
  0.0 90.3 %conv_module_back.1 = bf16[512,1024]{1,0:T(8,128)(2,1)} custom-call(bf16[512,1024]{1,0:T(8,128)(2,1)} %bitcast.9, bf16[64,16,1024]{2,1,0:T(8,128)(2,1)} %bitcast.8, bf16[1024,2048]{1,0:T(8,128)(2,1)} %w_in_hbm.1, bf16[1024,1024]{1,0:T(8,128)(2,1)} %w_out_hbm.1, s32[1,64]{1,0:T(1,128)} %slot_ref.1, s32[1,262]{1,0:T(1,128)} %utt_ref.1, f32[1,1024]{1,0:T(1,128)} %bitcast.10, ...), custom_call_target="tpu_custom_call" | custom-call | tf_op jit(solution)/shard_map/conv_module_back/pallas_call | solution.py:575
  90.3 2.3 %copy.13 = bf16[1,512,1024]{2,1,0:T(8,128)(2,1)} copy(bf16[1,512,1024]{2,1,0:T(8,128)(2,1)} %bitcast.7) | data formatting | bytes 2097152

commit v2 on v1

--- a/solution.py
+++ b/solution.py
@@ -28,7 +28,7 @@
 LANES = 128
 COLS = C // LANES
 ROWS = 128
-WIN = 6
+WIN = 16
 SENDS = SHARDS - 1
 ALL_FRAMES = float(FRAMES * SHARDS * NX)
 NT = (((1,), (1,)), ((), ()))
@@ -50,7 +50,7 @@
     dw_ref,
     bn_gain_ref,
     bn_bias_ref,
-    out_hbm,
+    out_ref,
     enc,
     llm,
     w_in,
@@ -81,7 +81,6 @@
     inc,
     d_mixed,
     h_buf,
-    out_buf,
     ar_src,
     ar_s,
     ar_xy,
@@ -96,7 +95,7 @@
     halo_recv,
     ar_send,
     ar_recv,
-    out_sem,
+    lines_in,
 ):
     sec = lax.axis_index("sec")
     tm = lax.axis_index("tm")
@@ -142,17 +141,9 @@
     ]
 
     barrier = pltpu.get_barrier_semaphore()
-
-    def greet(i, carry):
-        s_at, z_at, y_at = partner(i)
-        pl.semaphore_signal(
-            barrier, inc=1, device_id=place(s_at, z_at, y_at, dp), device_id_type=MESH
-        )
-        return carry
-
-    lax.fori_loop(0, SENDS, greet, 0)
-    others = [p for p, keep in zip(cross, [i != 0 for j in (2, 1, 3, 0) for i in (2, 1, 3, 0) if (i, j) != (0, 0)]) if keep]
-    for p in others:
+    x_line = [(sec, z, y, wrap(dp + i, NX)) for i in (2, 1, 3)]
+    greeted = line + plane + x_line
+    for p in greeted:
         pl.semaphore_signal(barrier, inc=1, device_id=place(*p), device_id_type=MESH)
 
     slot_row = slot_ref[...]
@@ -179,7 +170,10 @@
     lax.fori_loop(0, SHARDS, pack, 0)
     recv[me] = send[me]
 
-    pl.semaphore_wait(barrier, SENDS + len(others))
+    pl.semaphore_wait(barrier, len(greeted))
+    for p in plane:
+        pl.semaphore_signal(lines_in, inc=1, device_id=place(*p), device_id_type=MESH)
+    pl.semaphore_wait(lines_in, len(plane))
 
     def spread(partners, source, target_of, s_sem, r_sem):
         for i, p in enumerate(partners):
@@ -204,34 +198,44 @@
             device_id_type=MESH,
         )
 
-    def first(i, carry):
-        block_copy(i).start()
-        return carry
-
-    lax.fori_loop(0, WIN, first, 0)
-    sent = [WIN]
-
-    def pump_one(i):
-        block_copy(i - WIN).wait_send()
-        block_copy(i).start()
-
-    def pump(count):
-        low = sent[0]
-        high = min(SENDS, low + count)
-        sent[0] = high
+    started = [0]
+    ended = [0]
+
+    def begin(count):
+        low, high = started[0], min(SENDS, started[0] + count)
+        started[0] = high
+        assert high - ended[0] <= WIN
+
+        def step(i, carry):
+            block_copy(i).start()
+            return carry
+
         if high > low:
-
-            def step(i, carry):
-                pump_one(i)
-                return carry
-
             lax.fori_loop(low, high, step, 0)
 
-    def pumped(count):
-        low = sent[0]
-        assert low + count <= SENDS
-        sent[0] = low + count
-        return low
+    def settle(left):
+        low, high = ended[0], max(ended[0], started[0] - left)
+        ended[0] = high
+
+        def step(i, carry):
+            block_copy(i).wait_send()
+            return carry
+
+        if high > low:
+            lax.fori_loop(low, high, step, 0)
+
+    def reserve(count):
+        first = (ended[0], started[0])
+        ended[0] += count
+        started[0] += count
+        assert started[0] <= SENDS
+        return first
+
+    def pump(first, i):
+        block_copy(first[0] + i).wait_send()
+        block_copy(first[1] + i).start()
+
+    begin(8)
 
     loads[1].wait()
     gain = ln_gain_ref[...]
@@ -250,23 +254,22 @@
         return carry
 
     lax.fori_loop(0, 8, norm, 0)
-    pump(2)
+    begin(2)
 
     loads[2].wait()
-    low = pumped(8)
+    moved = reserve(4)
 
     def project(n, carry):
         at = pl.ds(pl.multiple_of(n * 256, 256), 256)
         gate_at = pl.ds(pl.multiple_of(C + n * 256, 256), 256)
         lin = jnp.dot(normed[...], w_in[:, at], preferred_element_type=F32)
         gate = jnp.dot(normed[...], w_in[:, gate_at], preferred_element_type=F32)
-        pump_one(low + 2 * n)
+        pump(moved, n)
         s = jax.nn.sigmoid(gate)
         mixed = lin * s
         sig[:, at] = s
         dsig[:, at] = mixed * (1.0 - s)
         gated[pl.ds(PAD, FRAMES), at] = mixed.astype(BF16).astype(F32)
-        pump_one(low + 2 * n + 1)
         return carry
 
     lax.fori_loop(0, 4, project, 0)
@@ -295,7 +298,9 @@
         wait_bytes(buf.at[pl.ds(0, PAD)], halo_send.at[k, 0])
         wait_bytes(buf.at[pl.ds(0, PAD)], halo_send.at[k, 1])
 
+    settle(6)
     edges(gated, 0)
+    begin(6)
 
     wait_bytes(ids_line.at[pl.ds(0, NZ - 1)], ids_recv.at[0])
     for j in range(NZ):
@@ -333,10 +338,9 @@
         return carry
 
     lax.fori_loop(0, FRAMES // ROWS, mark, 0)
-    pump(5)
     edges_in(gated, 0)
 
-    low_conv = pumped(8)
+    moved_conv = reserve(8)
 
     def convolve(c, carry):
         cols = pl.ds(pl.multiple_of(c * LANES, LANES), LANES)
@@ -356,12 +360,10 @@
             second_sum = second_sum + jnp.sum(total * total, axis=0, keepdims=True)
         ar_src[0, 0, 0, pl.ds(c, 1), :] = first_sum
         ar_src[0, 0, 1, pl.ds(c, 1), :] = second_sum
-        pump_one(low_conv + c)
+        pump(moved_conv, c)
         return carry
 
     lax.fori_loop(0, COLS, convolve, 0)
-    edges(conv, 1)
-
     groups = ((mate, ar_s), (cross, ar_xy), (line, ar_z))
 
     def sum_send(k, step):
@@ -387,9 +389,15 @@
         for step, (partners, target) in enumerate(groups):
             wait_bytes(target.at[k, pl.ds(0, len(partners))], ar_send.at[k, step])
 
-    for step, count in ((0, 1), (1, 7), (2, 7)):
+    settle(4)
+    sum_send(0, 0)
+    edges(conv, 1)
+    begin(7)
+    sum_recv(0, 0)
+    for step in (1, 2):
+        settle(4)
         sum_send(0, step)
-        pump(count)
+        begin(8)
         sum_recv(0, step)
 
     wait_bytes(ids_all.at[pl.ds(0, 7)], ids_recv.at[1])
@@ -404,16 +412,12 @@
     edges_in(conv, 1)
     edges_out(conv, 1)
 
-    low_bn = pumped(8)
+    moved_bn = reserve(8)
 
     def bn_scales(c):
         bn_mean = ar_src[0, 3, 0, pl.ds(c, 1), :] / ALL_FRAMES
         bn_var = ar_src[0, 3, 1, pl.ds(c, 1), :] / ALL_FRAMES - bn_mean * bn_mean
         return bn_mean, lax.rsqrt(bn_var + EPS)
-
-    def transposed(source, c, r, window_of):
-        taps = dw_ref[:, pl.ds(pl.multiple_of(c * LANES, LANES), LANES)]
-        return taps
 
     def normalise(c, carry):
         cols = pl.ds(pl.multiple_of(c * LANES, LANES), LANES)
@@ -439,13 +443,15 @@
                 z_total = z_total + weight * window[HALF + j : HALF + j + ROWS]
             ones_t[rows, cols] = ones_total
             z_t[rows, cols] = z_total
-        pump_one(low_bn + c)
+        pump(moved_bn, c)
         return carry
 
     lax.fori_loop(0, COLS, normalise, 0)
     src_copy.wait()
     loads[3].wait()
-    pump(SENDS)
+    settle(WIN - (SENDS - started[0]))
+    begin(SENDS)
+    assert started[0] == SENDS
 
     wait_bytes(recv.at[pl.ds(0, SENDS)], a2a_recv)
 
@@ -455,19 +461,17 @@
 
     lax.fori_loop(0, NBE, gather, 0)
 
-    def back(n, carry):
-        at = pl.ds(pl.multiple_of(n * 256, 256), 256)
+    for n in range(4):
+        at = slice(n * 256, n * 256 + 256)
         grad = lax.dot_general(inc[...], w_out[at, :], NT, preferred_element_type=F32)
         grad = grad * swish[:, at]
-        d_pre[pl.ds(PAD, FRAMES), at] = grad
+        d_pre[PAD : PAD + FRAMES, at] = grad
         first_sum = jnp.sum(grad, axis=0, keepdims=True)
-        cross_sum = jnp.sum(grad * conv[pl.ds(PAD, FRAMES), at], axis=0, keepdims=True)
+        cross_sum = jnp.sum(grad * conv[PAD : PAD + FRAMES, at], axis=0, keepdims=True)
         for j in range(2):
-            ar_src[1, 0, 0, pl.ds(2 * n + j, 1), :] = first_sum[:, j * LANES : (j + 1) * LANES]
-            ar_src[1, 0, 1, pl.ds(2 * n + j, 1), :] = cross_sum[:, j * LANES : (j + 1) * LANES]
-        return carry
-
-    lax.fori_loop(0, 4, back, 0)
+            c = 2 * n + j
+            ar_src[1, 0, 0, c : c + 1, :] = first_sum[:, j * LANES : (j + 1) * LANES]
+            ar_src[1, 0, 1, c : c + 1, :] = cross_sum[:, j * LANES : (j + 1) * LANES]
 
     def conv_back(c, carry):
         cols = pl.ds(pl.multiple_of(c * LANES, LANES), LANES)
@@ -511,46 +515,30 @@
 
     lax.fori_loop(0, COLS, assemble, 0)
 
-    def unproject(n, carry):
-        at = pl.ds(pl.multiple_of(n * 256, 256), 256)
+    for n in range(4):
+        at = slice(n * 256, n * 256 + 256)
         grad = lax.dot_general(d_mixed[...], w_in[at, :], NT, preferred_element_type=F32)
         h_buf[:, at] = grad * ln_gain_ref[:, at]
-        return carry
-
-    lax.fori_loop(0, 4, unproject, 0)
-
-    stores = []
-    for r in range(4):
-        rows = pl.ds(r * ROWS, ROWS)
-
-        def finish(k, carry, r=r):
-            part = pl.ds(pl.multiple_of(r * ROWS + k * 32, 32), 32)
-            h = h_buf[part, :]
-            hat = x_hat[part, :]
-            mean = jnp.mean(h, axis=1, keepdims=True)
-            along = jnp.mean(h * hat, axis=1, keepdims=True)
-            scale = rstd[part, 0:1]
-            out_buf[part, :] = (inc[part, :].astype(F32) + scale * (h - mean - hat * along)).astype(BF16)
-            return carry
-
-        lax.fori_loop(0, 4, finish, 0)
-        store = pltpu.make_async_copy(out_buf.at[rows], out_hbm.at[rows], out_sem.at[r])
-        store.start()
-        stores.append(store)
-
-    def drain(i, carry):
-        block_copy(i).wait_send()
-        return carry
-
-    lax.fori_loop(SENDS - WIN, SENDS, drain, 0)
+
+    def finish(k, carry):
+        part = pl.ds(pl.multiple_of(k * 32, 32), 32)
+        h = h_buf[part, :]
+        hat = x_hat[part, :]
+        mean = jnp.mean(h, axis=1, keepdims=True)
+        along = jnp.mean(h * hat, axis=1, keepdims=True)
+        scale = rstd[part, 0:1]
+        out_ref[part, :] = (inc[part, :].astype(F32) + scale * (h - mean - hat * along)).astype(BF16)
+        return carry
+
+    lax.fori_loop(0, FRAMES // 32, finish, 0)
+
+    settle(0)
     wait_bytes(ids_line.at[pl.ds(0, NZ - 1)], ids_send.at[0])
     wait_bytes(ids_all.at[pl.ds(0, 7)], ids_send.at[1])
     edges_out(gated, 0)
     edges_out(d_pre, 2)
     sum_done(0)
     sum_done(1)
-    for store in stores:
-        store.wait()
 
 
 def local(
@@ -576,7 +564,7 @@
         kernel,
         out_shape=jax.ShapeDtypeStruct((FRAMES, C), BF16),
         in_specs=[hbm] * 4 + [vmem] * 7,
-        out_specs=hbm,
+        out_specs=vmem,
         scratch_shapes=[
             pltpu.VMEM((FRAMES, C), BF16),
             blocks,
@@ -608,7 +596,6 @@
             pltpu.VMEM((FRAMES, C), BF16),
             pltpu.VMEM((FRAMES, 2 * C), BF16),
             full,
-            pltpu.VMEM((FRAMES, C), BF16),
             pltpu.VMEM((2, 4, 2, COLS, LANES), F32),
             pltpu.VMEM((2, 1, 2, COLS, LANES), F32),
             pltpu.VMEM((2, 15, 2, COLS, LANES), F32),
@@ -623,7 +610,7 @@
             dma((3, 2)),
             dma((2, 3)),
             dma((2, 3)),
-            dma((4,)),
+            pltpu.SemaphoreType.REGULAR,
         ],
         compiler_params=pltpu.CompilerParams(
             collective_id=1, has_side_effects=True, vmem_limit_bytes=56 << 20

time: 92.7 us -> 88.9 us (0.959)
  Pallas kernels: 90.3 us -> 86.4 us
    pallas_call x1, Pallas kernels: 90.3 us -> 86.4 us  [local(): pl.pallas_call(kernel, out_shape=jax.ShapeDtypeStruct((FRAMES, C), BF16),...]
where the time goes in v2:
time: 88.9 us; the launch traced here: 88.7 us
  Pallas kernels  86.4 us (97%)
  local copies, waits for them, and re-layouts  2.26 us (3%)
    pallas_call x1, Pallas kernels, local(): pl.pallas_call(kernel, out_shape=jax.ShapeDtypeStruct((FRAMES, C), BF16),...  86.4 us
    unnamed x1, local copies, waits for them, and re-layouts  2.26 us

profile of v2, /device:TPU:1, one launch (start us, length us, event | category | flops | bytes accessed | tf_op | source)
XLA Modules:
  0.0 88.7 jit_solution(16873156270202527065)
XLA Ops:
  0.0 86.4 %conv_module_back.1 = bf16[512,1024]{1,0:T(8,128)(2,1)} custom-call(bf16[512,1024]{1,0:T(8,128)(2,1)} %bitcast.9, bf16[64,16,1024]{2,1,0:T(8,128)(2,1)} %bitcast.8, bf16[1024,2048]{1,0:T(8,128)(2,1)} %w_in_hbm.1, bf16[1024,1024]{1,0:T(8,128)(2,1)} %w_out_hbm.1, s32[1,64]{1,0:T(1,128)} %slot_ref.1, s32[1,262]{1,0:T(1,128)} %utt_ref.1, f32[1,1024]{1,0:T(1,128)} %bitcast.10, ...), custom_call_target="tpu_custom_call" | custom-call | tf_op jit(solution)/shard_map/conv_module_back/pallas_call | solution.py:563
  86.4 2.3 %copy.13 = bf16[1,512,1024]{2,1,0:T(8,128)(2,1)} copy(bf16[1,512,1024]{2,1,0:T(8,128)(2,1)} %bitcast.7) | data formatting | bytes 2097152

commit v3 on v2

--- a/solution.py
+++ b/solution.py
@@ -21,6 +21,9 @@
 HALF = 4
 PAD = 8
 EXT = FRAMES + 2 * PAD
+EDGE = 16
+THIRD = EXT // 3
+WIDE = FRAMES + 2 * EDGE
 BLK = 16
 NBE = 32
 UTT = 262
@@ -28,7 +31,7 @@
 LANES = 128
 COLS = C // LANES
 ROWS = 128
-WIN = 16
+WIN = 20
 SENDS = SHARDS - 1
 ALL_FRAMES = float(FRAMES * SHARDS * NX)
 NT = (((1,), (1,)), ((), ()))
@@ -50,7 +53,7 @@
     dw_ref,
     bn_gain_ref,
     bn_bias_ref,
-    out_ref,
+    out_hbm,
     enc,
     llm,
     w_in,
@@ -80,7 +83,7 @@
     d_pre,
     inc,
     d_mixed,
-    h_buf,
+    out_buf,
     ar_src,
     ar_s,
     ar_xy,
@@ -95,6 +98,7 @@
     halo_recv,
     ar_send,
     ar_recv,
+    out_sem,
     lines_in,
 ):
     sec = lax.axis_index("sec")
@@ -109,7 +113,7 @@
 
     loads = []
     for k, (source, target) in enumerate(
-        ((llm_hbm, llm), (enc_hbm, enc), (w_in_hbm, w_in), (w_out_hbm, w_out))
+        ((llm_hbm, llm), (enc_hbm, enc.at[pl.ds(EDGE, FRAMES)]), (w_in_hbm, w_in), (w_out_hbm, w_out))
     ):
         load = pltpu.make_async_copy(source, target, load_sem.at[k])
         load.start()
@@ -184,6 +188,32 @@
     def wait_bytes(ref, sem):
         pltpu.make_async_copy(ref, ref, sem).wait()
 
+    before = wrap(me + SHARDS - 1, SHARDS)
+    after = wrap(me + 1, SHARDS)
+
+    def edges(buf, rows, k):
+        for j, (to, start, end) in enumerate(
+            ((after, FRAMES, 0), (before, rows, rows + FRAMES))
+        ):
+            pltpu.make_async_remote_copy(
+                buf.at[pl.ds(start, rows)],
+                buf.at[pl.ds(end, rows)],
+                halo_send.at[k, j],
+                halo_recv.at[k, j],
+                device_id={"sec": to // (NZ * NY), "tm": lax.rem(to, NZ * NY), "dp": dp},
+                device_id_type=MESH,
+            ).start()
+
+    def edges_in(buf, rows, k):
+        wait_bytes(buf.at[pl.ds(0, rows)], halo_recv.at[k, 0])
+        wait_bytes(buf.at[pl.ds(0, rows)], halo_recv.at[k, 1])
+
+    def edges_out(buf, rows, k):
+        wait_bytes(buf.at[pl.ds(0, rows)], halo_send.at[k, 0])
+        wait_bytes(buf.at[pl.ds(0, rows)], halo_send.at[k, 1])
+
+    loads[1].wait()
+    edges(enc, EDGE, 0)
     spread(line, ids_line.at[z], lambda i: ids_line.at[z], ids_send.at[0], ids_recv.at[0])
 
     def block_copy(i):
@@ -235,26 +265,63 @@
         block_copy(first[0] + i).wait_send()
         block_copy(first[1] + i).start()
 
-    begin(8)
-
-    loads[1].wait()
+    begin(10)
+
     gain = ln_gain_ref[...]
     bias = ln_bias_ref[...]
 
-    def norm(r, carry):
-        rows = pl.ds(pl.multiple_of(r * 64, 64), 64)
-        values = enc[rows, :].astype(F32)
+    def norm_rows(values):
+        values = values.astype(F32)
         mean = jnp.mean(values, axis=1, keepdims=True)
         centred = values - mean
         scale = lax.rsqrt(jnp.mean(centred * centred, axis=1, keepdims=True) + EPS)
         hat = centred * scale
+        return hat, scale, (hat * gain + bias).astype(BF16)
+
+    def norm(r, carry):
+        rows = pl.ds(pl.multiple_of(r * 64, 64), 64)
+        wide_rows = pl.ds(pl.multiple_of(r * 64 + EDGE, EDGE), 64)
+        hat, scale, out = norm_rows(enc[wide_rows, :])
         rstd[rows, :] = jnp.broadcast_to(scale, (64, LANES))
         x_hat[rows, :] = hat
-        normed[rows, :] = (hat * gain + bias).astype(BF16)
+        normed[wide_rows, :] = out
         return carry
 
     lax.fori_loop(0, 8, norm, 0)
-    begin(2)
+
+    utt_pad[...] = jnp.zeros((8, UTT_PAD), I32)
+    utt_pad[0:1, 0:UTT] = utt_ref[...]
+    lengths = utt_pad[...].astype(F32).astype(BF16)
+    upper = (
+        lax.broadcasted_iota(I32, (UTT_PAD, UTT_PAD), 0)
+        <= lax.broadcasted_iota(I32, (UTT_PAD, UTT_PAD), 1)
+    ).astype(F32).astype(BF16)
+    ends = jnp.dot(lengths, upper, preferred_element_type=F32)[0:1, :]
+
+    def number(r, carry):
+        rows = pl.ds(pl.multiple_of(r * 136, 8), 136)
+        position = lax.broadcasted_iota(I32, (136, 1), 0) + (r * 136 + me * FRAMES - EDGE)
+        position_f = position.astype(F32)
+        count = jnp.sum((position_f >= ends).astype(F32), axis=1, keepdims=True)
+        inside = (position >= 0) & (position < SHARDS * FRAMES)
+        seg[rows, :] = jnp.broadcast_to(jnp.where(inside, count, -1.0), (136, LANES))
+        return carry
+
+    lax.fori_loop(0, WIDE // 136, number, 0)
+
+    def mark(r, carry):
+        window = seg[pl.ds(pl.multiple_of(r * THIRD, 16), THIRD + 2 * PAD), :]
+        own = window[PAD : PAD + THIRD]
+        rows = pl.ds(pl.multiple_of(r * THIRD, 16), THIRD)
+        for j in range(TAPS):
+            masks[j, rows, :] = (window[HALF + j : HALF + j + THIRD] == own).astype(F32)
+        return carry
+
+    lax.fori_loop(0, EXT // THIRD, mark, 0)
+
+    edges_in(enc, EDGE, 0)
+    for start in (0, EDGE + FRAMES):
+        normed[start : start + EDGE, :] = norm_rows(enc[start : start + EDGE, :])[2]
 
     loads[2].wait()
     moved = reserve(4)
@@ -267,78 +334,12 @@
         pump(moved, n)
         s = jax.nn.sigmoid(gate)
         mixed = lin * s
-        sig[:, at] = s
-        dsig[:, at] = mixed * (1.0 - s)
-        gated[pl.ds(PAD, FRAMES), at] = mixed.astype(BF16).astype(F32)
+        sig[:, at] = s[EDGE : EDGE + FRAMES]
+        dsig[:, at] = (mixed * (1.0 - s))[EDGE : EDGE + FRAMES]
+        gated[:, at] = mixed.astype(BF16).astype(F32)
         return carry
 
     lax.fori_loop(0, 4, project, 0)
-
-    before = wrap(me + SHARDS - 1, SHARDS)
-    after = wrap(me + 1, SHARDS)
-
-    def edges(buf, k):
-        for j, (to, start, end) in enumerate(
-            ((after, FRAMES, 0), (before, PAD, PAD + FRAMES))
-        ):
-            pltpu.make_async_remote_copy(
-                buf.at[pl.ds(start, PAD)],
-                buf.at[pl.ds(end, PAD)],
-                halo_send.at[k, j],
-                halo_recv.at[k, j],
-                device_id={"sec": to // (NZ * NY), "tm": lax.rem(to, NZ * NY), "dp": dp},
-                device_id_type=MESH,
-            ).start()
-
-    def edges_in(buf, k):
-        wait_bytes(buf.at[pl.ds(0, PAD)], halo_recv.at[k, 0])
-        wait_bytes(buf.at[pl.ds(PAD + FRAMES, PAD)], halo_recv.at[k, 1])
-
-    def edges_out(buf, k):
-        wait_bytes(buf.at[pl.ds(0, PAD)], halo_send.at[k, 0])
-        wait_bytes(buf.at[pl.ds(0, PAD)], halo_send.at[k, 1])
-
-    settle(6)
-    edges(gated, 0)
-    begin(6)
-
-    wait_bytes(ids_line.at[pl.ds(0, NZ - 1)], ids_recv.at[0])
-    for j in range(NZ):
-        ids_tile[j : j + 1, :] = ids_line[j]
-    here = sec * NY + y
-    ids_all[here] = ids_tile[...]
-    spread(plane, ids_tile, lambda i: ids_all.at[here], ids_send.at[1], ids_recv.at[1])
-
-    utt_pad[...] = jnp.zeros((8, UTT_PAD), I32)
-    utt_pad[0:1, 0:UTT] = utt_ref[...]
-    lengths = utt_pad[...].astype(F32).astype(BF16)
-    upper = (
-        lax.broadcasted_iota(I32, (UTT_PAD, UTT_PAD), 0)
-        <= lax.broadcasted_iota(I32, (UTT_PAD, UTT_PAD), 1)
-    ).astype(F32).astype(BF16)
-    ends = jnp.dot(lengths, upper, preferred_element_type=F32)[0:1, :]
-
-    def number(r, carry):
-        rows = pl.ds(pl.multiple_of(r * 48, 8), 48)
-        position = lax.broadcasted_iota(I32, (48, 1), 0) + (r * 48 + me * FRAMES - PAD)
-        position_f = position.astype(F32)
-        count = jnp.sum((position_f >= ends).astype(F32), axis=1, keepdims=True)
-        inside = (position >= 0) & (position < SHARDS * FRAMES)
-        seg[rows, :] = jnp.broadcast_to(jnp.where(inside, count, -1.0), (48, LANES))
-        return carry
-
-    lax.fori_loop(0, EXT // 48, number, 0)
-
-    def mark(r, carry):
-        window = seg[pl.ds(pl.multiple_of(r * ROWS, ROWS), ROWS + 2 * PAD), :]
-        own = window[PAD : PAD + ROWS]
-        rows = pl.ds(pl.multiple_of(r * ROWS, ROWS), ROWS)
-        for j in range(TAPS):
-            masks[j, rows, :] = (window[HALF + j : HALF + j + ROWS] == own).astype(F32)
-        return carry
-
-    lax.fori_loop(0, FRAMES // ROWS, mark, 0)
-    edges_in(gated, 0)
 
     moved_conv = reserve(8)
 
@@ -347,23 +348,25 @@
         taps = dw_ref[:, cols]
         first_sum = jnp.zeros((1, LANES), F32)
         second_sum = jnp.zeros((1, LANES), F32)
-        for r in range(FRAMES // ROWS):
-            window = gated[r * ROWS : r * ROWS + ROWS + 2 * PAD, cols]
-            total = jnp.zeros((ROWS, LANES), F32)
+        for r in range(EXT // THIRD):
+            window = gated[r * THIRD : r * THIRD + THIRD + 2 * PAD, cols]
+            total = jnp.zeros((THIRD, LANES), F32)
             for k in range(TAPS):
-                part = window[HALF + k : HALF + k + ROWS]
+                part = window[HALF + k : HALF + k + THIRD]
                 if k != HALF:
-                    part = part * masks[k, r * ROWS : r * ROWS + ROWS, :]
+                    part = part * masks[k, r * THIRD : r * THIRD + THIRD, :]
                 total = total + taps[k : k + 1, :] * part
-            conv[PAD + r * ROWS : PAD + r * ROWS + ROWS, cols] = total
-            first_sum = first_sum + jnp.sum(total, axis=0, keepdims=True)
-            second_sum = second_sum + jnp.sum(total * total, axis=0, keepdims=True)
+            conv[r * THIRD : r * THIRD + THIRD, cols] = total
+            own = total[(PAD if r == 0 else 0) : (THIRD - PAD if r == EXT // THIRD - 1 else THIRD)]
+            first_sum = first_sum + jnp.sum(own, axis=0, keepdims=True)
+            second_sum = second_sum + jnp.sum(own * own, axis=0, keepdims=True)
         ar_src[0, 0, 0, pl.ds(c, 1), :] = first_sum
         ar_src[0, 0, 1, pl.ds(c, 1), :] = second_sum
         pump(moved_conv, c)
         return carry
 
     lax.fori_loop(0, COLS, convolve, 0)
+
     groups = ((mate, ar_s), (cross, ar_xy), (line, ar_z))
 
     def sum_send(k, step):
@@ -389,16 +392,26 @@
         for step, (partners, target) in enumerate(groups):
             wait_bytes(target.at[k, pl.ds(0, len(partners))], ar_send.at[k, step])
 
-    settle(4)
+    settle(8)
     sum_send(0, 0)
-    edges(conv, 1)
-    begin(7)
+    begin(8)
+
+    wait_bytes(ids_line.at[pl.ds(0, NZ - 1)], ids_recv.at[0])
+    for j in range(NZ):
+        ids_tile[j : j + 1, :] = ids_line[j]
+    here = sec * NY + y
+    ids_all[here] = ids_tile[...]
+    spread(plane, ids_tile, lambda i: ids_all.at[here], ids_send.at[1], ids_recv.at[1])
+
     sum_recv(0, 0)
-    for step in (1, 2):
-        settle(4)
-        sum_send(0, step)
-        begin(8)
-        sum_recv(0, step)
+    settle(6)
+    sum_send(0, 1)
+    begin(12)
+    sum_recv(0, 1)
+    settle(6)
+    sum_send(0, 2)
+    begin(12)
+    sum_recv(0, 2)
 
     wait_bytes(ids_all.at[pl.ds(0, 7)], ids_recv.at[1])
     ids = ids_all[...].reshape(64, LANES)
@@ -408,9 +421,6 @@
     row_buf[1:2, :] = jnp.sum(jnp.where(mine == lane, source, 0), axis=0, keepdims=True)
     src_copy = pltpu.make_async_copy(row_buf.at[pl.ds(1, 1)], src_tbl, tbl_sem.at[1])
     src_copy.start()
-
-    edges_in(conv, 1)
-    edges_out(conv, 1)
 
     moved_bn = reserve(8)
 
@@ -438,7 +448,7 @@
             ones_total = jnp.zeros((ROWS, LANES), F32)
             z_total = jnp.zeros((ROWS, LANES), F32)
             for j in range(TAPS):
-                weight = (taps[TAPS - 1 - j : TAPS - j, :] * factor) * masks[j, rows, :]
+                weight = (taps[TAPS - 1 - j : TAPS - j, :] * factor) * masks[j, PAD + r * ROWS : PAD + r * ROWS + ROWS, :]
                 ones_total = ones_total + weight
                 z_total = z_total + weight * window[HALF + j : HALF + j + ROWS]
             ones_t[rows, cols] = ones_total
@@ -485,16 +495,16 @@
             for j in range(TAPS):
                 part = window[HALF + j : HALF + j + ROWS]
                 if j != HALF:
-                    part = part * masks[j, rows, :]
+                    part = part * masks[j, PAD + r * ROWS : PAD + r * ROWS + ROWS, :]
                 total = total + taps[TAPS - 1 - j : TAPS - j, :] * part
             d_t[rows, cols] = total
         return carry
 
     sum_send(1, 0)
-    edges(d_pre, 2)
+    edges(d_pre, PAD, 1)
     sum_recv(1, 0)
     sum_send(1, 1)
-    edges_in(d_pre, 2)
+    edges_in(d_pre, PAD, 1)
     lax.fori_loop(0, COLS // 2, conv_back, 0)
     sum_recv(1, 1)
     sum_send(1, 2)
@@ -515,30 +525,31 @@
 
     lax.fori_loop(0, COLS, assemble, 0)
 
-    for n in range(4):
-        at = slice(n * 256, n * 256 + 256)
-        grad = lax.dot_general(d_mixed[...], w_in[at, :], NT, preferred_element_type=F32)
-        h_buf[:, at] = grad * ln_gain_ref[:, at]
-
-    def finish(k, carry):
-        part = pl.ds(pl.multiple_of(k * 32, 32), 32)
-        h = h_buf[part, :]
-        hat = x_hat[part, :]
+    stores = []
+    for m in range(2):
+        rows = slice(m * 256, m * 256 + 256)
+        h = lax.dot_general(d_mixed[rows, :], w_in[...], NT, preferred_element_type=F32)
+        h = h * gain
+        hat = x_hat[rows, :]
         mean = jnp.mean(h, axis=1, keepdims=True)
         along = jnp.mean(h * hat, axis=1, keepdims=True)
-        scale = rstd[part, 0:1]
-        out_ref[part, :] = (inc[part, :].astype(F32) + scale * (h - mean - hat * along)).astype(BF16)
-        return carry
-
-    lax.fori_loop(0, FRAMES // 32, finish, 0)
+        scale = rstd[rows, 0:1]
+        out_buf[rows, :] = (inc[rows, :].astype(F32) + scale * (h - mean - hat * along)).astype(BF16)
+        store = pltpu.make_async_copy(
+            out_buf.at[pl.ds(m * 256, 256)], out_hbm.at[pl.ds(m * 256, 256)], out_sem.at[m]
+        )
+        store.start()
+        stores.append(store)
 
     settle(0)
     wait_bytes(ids_line.at[pl.ds(0, NZ - 1)], ids_send.at[0])
     wait_bytes(ids_all.at[pl.ds(0, 7)], ids_send.at[1])
-    edges_out(gated, 0)
-    edges_out(d_pre, 2)
+    edges_out(enc, EDGE, 0)
+    edges_out(d_pre, PAD, 1)
     sum_done(0)
     sum_done(1)
+    for store in stores:
+        store.wait()
 
 
 def local(
@@ -564,9 +575,9 @@
         kernel,
         out_shape=jax.ShapeDtypeStruct((FRAMES, C), BF16),
         in_specs=[hbm] * 4 + [vmem] * 7,
-        out_specs=vmem,
+        out_specs=hbm,
         scratch_shapes=[
-            pltpu.VMEM((FRAMES, C), BF16),
+            pltpu.VMEM((WIDE, C), BF16),
             blocks,
             pltpu.VMEM((C, 2 * C), BF16),
             pltpu.VMEM((C, C), BF16),
@@ -579,14 +590,14 @@
             pltpu.VMEM((NZ, LANES), I32),
             pltpu.VMEM((8, NZ, LANES), I32),
             pltpu.VMEM((8, UTT_PAD), I32),
-            pltpu.VMEM((EXT, LANES), F32),
-            pltpu.VMEM((TAPS, FRAMES, LANES), F32),
+            pltpu.VMEM((WIDE, LANES), F32),
+            pltpu.VMEM((TAPS, EXT, LANES), F32),
             full,
             pltpu.VMEM((FRAMES, LANES), F32),
-            pltpu.VMEM((FRAMES, C), BF16),
+            pltpu.VMEM((WIDE, C), BF16),
             full,
             full,
-            wide,
+            pltpu.VMEM((WIDE, C), F32),
             wide,
             full,
             full,
@@ -595,7 +606,7 @@
             wide,
             pltpu.VMEM((FRAMES, C), BF16),
             pltpu.VMEM((FRAMES, 2 * C), BF16),
-            full,
+            pltpu.VMEM((FRAMES, C), BF16),
             pltpu.VMEM((2, 4, 2, COLS, LANES), F32),
             pltpu.VMEM((2, 1, 2, COLS, LANES), F32),
             pltpu.VMEM((2, 15, 2, COLS, LANES), F32),
@@ -606,10 +617,11 @@
             dma,
             dma((2,)),
             dma((2,)),
-            dma((3, 2)),
-            dma((3, 2)),
+            dma((2, 2)),
+            dma((2, 2)),
             dma((2, 3)),
             dma((2, 3)),
+            dma((2,)),
             pltpu.SemaphoreType.REGULAR,
         ],
         compiler_params=pltpu.CompilerParams(

time: 88.9 us -> 84.1 us (0.946)
  Pallas kernels: 86.4 us -> 81.6 us
    pallas_call x1, Pallas kernels: 86.4 us -> 81.6 us  [local(): pl.pallas_call(kernel, out_shape=jax.ShapeDtypeStruct((FRAMES, C), BF16),...]
where the time goes in v3:
time: 84.1 us; the launch traced here: 83.9 us
  Pallas kernels  81.6 us (97%)
  local copies, waits for them, and re-layouts  2.26 us (3%)
    pallas_call x1, Pallas kernels, local(): pl.pallas_call(kernel, out_shape=jax.ShapeDtypeStruct((FRAMES, C), BF16),...  81.6 us
    unnamed x1, local copies, waits for them, and re-layouts  2.26 us

profile of v3, /device:TPU:1, one launch (start us, length us, event | category | flops | bytes accessed | tf_op | source)
XLA Modules:
  0.0 83.9 jit_solution(13809632866009663044)
XLA Ops:
  0.0 81.6 %conv_module_back.1 = bf16[512,1024]{1,0:T(8,128)(2,1)} custom-call(bf16[512,1024]{1,0:T(8,128)(2,1)} %bitcast.9, bf16[64,16,1024]{2,1,0:T(8,128)(2,1)} %bitcast.8, bf16[1024,2048]{1,0:T(8,128)(2,1)} %w_in_hbm.1, bf16[1024,1024]{1,0:T(8,128)(2,1)} %w_out_hbm.1, s32[1,64]{1,0:T(1,128)} %slot_ref.1, s32[1,262]{1,0:T(1,128)} %utt_ref.1, f32[1,1024]{1,0:T(1,128)} %bitcast.10, ...), custom_call_target="tpu_custom_call" | custom-call | tf_op jit(solution)/shard_map/conv_module_back/pallas_call | solution.py:574
  81.7 2.3 %copy.13 = bf16[1,512,1024]{2,1,0:T(8,128)(2,1)} copy(bf16[1,512,1024]{2,1,0:T(8,128)(2,1)} %bitcast.7) | data formatting | bytes 2097152

commit v4 on v3

--- a/solution.py
+++ b/solution.py
@@ -53,7 +53,7 @@
     dw_ref,
     bn_gain_ref,
     bn_bias_ref,
-    out_hbm,
+    out_ref,
     enc,
     llm,
     w_in,
@@ -83,7 +83,6 @@
     d_pre,
     inc,
     d_mixed,
-    out_buf,
     ar_src,
     ar_s,
     ar_xy,
@@ -98,7 +97,6 @@
     halo_recv,
     ar_send,
     ar_recv,
-    out_sem,
     lines_in,
 ):
     sec = lax.axis_index("sec")
@@ -265,7 +263,7 @@
         block_copy(first[0] + i).wait_send()
         block_copy(first[1] + i).start()
 
-    begin(10)
+    begin(6)
 
     gain = ln_gain_ref[...]
     bias = ln_bias_ref[...]
@@ -341,7 +339,7 @@
 
     lax.fori_loop(0, 4, project, 0)
 
-    moved_conv = reserve(8)
+    moved_conv = reserve(4)
 
     def convolve(c, carry):
         cols = pl.ds(pl.multiple_of(c * LANES, LANES), LANES)
@@ -362,7 +360,11 @@
             second_sum = second_sum + jnp.sum(own * own, axis=0, keepdims=True)
         ar_src[0, 0, 0, pl.ds(c, 1), :] = first_sum
         ar_src[0, 0, 1, pl.ds(c, 1), :] = second_sum
-        pump(moved_conv, c)
+
+        @pl.when(lax.rem(c, 2) == 0)
+        def _():
+            pump(moved_conv, c // 2)
+
         return carry
 
     lax.fori_loop(0, COLS, convolve, 0)
@@ -392,9 +394,9 @@
         for step, (partners, target) in enumerate(groups):
             wait_bytes(target.at[k, pl.ds(0, len(partners))], ar_send.at[k, step])
 
-    settle(8)
+    settle(4)
     sum_send(0, 0)
-    begin(8)
+    begin(7)
 
     wait_bytes(ids_line.at[pl.ds(0, NZ - 1)], ids_recv.at[0])
     for j in range(NZ):
@@ -404,13 +406,13 @@
     spread(plane, ids_tile, lambda i: ids_all.at[here], ids_send.at[1], ids_recv.at[1])
 
     sum_recv(0, 0)
-    settle(6)
+    settle(3)
     sum_send(0, 1)
-    begin(12)
+    begin(14)
     sum_recv(0, 1)
-    settle(6)
+    settle(3)
     sum_send(0, 2)
-    begin(12)
+    begin(14)
     sum_recv(0, 2)
 
     wait_bytes(ids_all.at[pl.ds(0, 7)], ids_recv.at[1])
@@ -459,7 +461,7 @@
     lax.fori_loop(0, COLS, normalise, 0)
     src_copy.wait()
     loads[3].wait()
-    settle(WIN - (SENDS - started[0]))
+    settle(max(0, WIN - (SENDS - started[0])))
     begin(SENDS)
     assert started[0] == SENDS
 
@@ -506,6 +508,11 @@
     sum_send(1, 1)
     edges_in(d_pre, PAD, 1)
     lax.fori_loop(0, COLS // 2, conv_back, 0)
+    settle(0)
+    wait_bytes(ids_line.at[pl.ds(0, NZ - 1)], ids_send.at[0])
+    wait_bytes(ids_all.at[pl.ds(0, 7)], ids_send.at[1])
+    edges_out(enc, EDGE, 0)
+    sum_done(0)
     sum_recv(1, 1)
     sum_send(1, 2)
     lax.fori_loop(COLS // 2, COLS, conv_back, 0)
@@ -525,7 +532,6 @@
 
     lax.fori_loop(0, COLS, assemble, 0)
 
-    stores = []
     for m in range(2):
         rows = slice(m * 256, m * 256 + 256)
         h = lax.dot_general(d_mixed[rows, :], w_in[...], NT, preferred_element_type=F32)
@@ -534,22 +540,10 @@
         mean = jnp.mean(h, axis=1, keepdims=True)
         along = jnp.mean(h * hat, axis=1, keepdims=True)
         scale = rstd[rows, 0:1]
-        out_buf[rows, :] = (inc[rows, :].astype(F32) + scale * (h - mean - hat * along)).astype(BF16)
-        store = pltpu.make_async_copy(
-            out_buf.at[pl.ds(m * 256, 256)], out_hbm.at[pl.ds(m * 256, 256)], out_sem.at[m]
-        )
-        store.start()
-        stores.append(store)
-
-    settle(0)
-    wait_bytes(ids_line.at[pl.ds(0, NZ - 1)], ids_send.at[0])
-    wait_bytes(ids_all.at[pl.ds(0, 7)], ids_send.at[1])
-    edges_out(enc, EDGE, 0)
+        out_ref[rows, :] = (inc[rows, :].astype(F32) + scale * (h - mean - hat * along)).astype(BF16)
+
     edges_out(d_pre, PAD, 1)
-    sum_done(0)
     sum_done(1)
-    for store in stores:
-        store.wait()
 
 
 def local(
@@ -566,7 +560,7 @@
     w_out,
 ):
     vmem = pl.BlockSpec(memory_space=pltpu.VMEM)
-    hbm = pl.BlockSpec(memory_space=pl.ANY)
+    hbm = pl.BlockSpec(memory_space=pltpu.HBM)
     dma = pltpu.SemaphoreType.DMA
     full = pltpu.VMEM((FRAMES, C), F32)
     wide = pltpu.VMEM((EXT, C), F32)
@@ -575,7 +569,7 @@
         kernel,
         out_shape=jax.ShapeDtypeStruct((FRAMES, C), BF16),
         in_specs=[hbm] * 4 + [vmem] * 7,
-        out_specs=hbm,
+        out_specs=vmem,
         scratch_shapes=[
             pltpu.VMEM((WIDE, C), BF16),
             blocks,
@@ -606,7 +600,6 @@
             wide,
             pltpu.VMEM((FRAMES, C), BF16),
             pltpu.VMEM((FRAMES, 2 * C), BF16),
-            pltpu.VMEM((FRAMES, C), BF16),
             pltpu.VMEM((2, 4, 2, COLS, LANES), F32),
             pltpu.VMEM((2, 1, 2, COLS, LANES), F32),
             pltpu.VMEM((2, 15, 2, COLS, LANES), F32),
@@ -621,11 +614,10 @@
             dma((2, 2)),
             dma((2, 3)),
             dma((2, 3)),
-            dma((2,)),
             pltpu.SemaphoreType.REGULAR,
         ],
         compiler_params=pltpu.CompilerParams(
-            collective_id=1, has_side_effects=True, vmem_limit_bytes=56 << 20
+            collective_id=1, has_side_effects=True, vmem_limit_bytes=52 << 20
         ),
         name="conv_module_back",
     )(

time: 84.1 us -> 88.1 us (1.048)
  local copies, waits for them, and re-layouts: 2.26 us -> 5.89 us
    unnamed x1 -> x15, local copies, waits for them, and re-layouts: 2.26 us -> 5.89 us
where the time goes in v4:
time: 88.1 us; the launch traced here: 87.8 us
  Pallas kernels  81.9 us (93%)
  local copies, waits for them, and re-layouts  5.89 us (7%)
    pallas_call x1, Pallas kernels, local(): pl.pallas_call(kernel, out_shape=jax.ShapeDtypeStruct((FRAMES, C), BF16),...  81.9 us
    unnamed x15, local copies, waits for them, and re-layouts  5.89 us

profile of v4, /device:TPU:1, one launch (start us, length us, event | category | flops | bytes accessed | tf_op | source)
XLA Modules:
  0.0 87.8 jit_solution(8188821270673193139)
XLA Ops:
  0.0 0.0 copy-start
  0.0 0.8 copy-done
  0.8 0.0 copy-start.1
  0.8 0.7 copy-done.1
  1.5 0.0 copy-start.2
  1.5 0.7 copy-done.2
  2.2 0.0 copy-start.3
  2.2 0.7 copy-done.3
  2.9 0.0 copy-start.4
  2.9 0.7 copy-done.4
  3.6 0.0 copy-start.5
  3.6 0.7 copy-done.5
  4.3 0.0 copy-start.6
  4.3 0.7 copy-done.6
  4.9 81.9 %conv_module_back.1 = bf16[512,1024]{1,0:T(8,128)(2,1)S(1)} custom-call(bf16[512,1024]{1,0:T(8,128)(2,1)} %bitcast.13, bf16[64,16,1024]{2,1,0:T(8,128)(2,1)} %bitcast.12, bf16[1024,2048]{1,0:T(8,128)(2,1)} %w_in_hbm.1, bf16[1024,1024]{1,0:T(8,128)(2,1)} %w_out_hbm.1, s32[1,64]{1,0:T(1,128)S(1)} %copy-done.6, s32[1,262]{1,0:T(1,128)S(1)} %copy-done.5, ...), custom_call_target="tpu_custom_call" | custom-call | tf_op jit(solution)/shard_map/conv_module_back/pallas_call | solution.py:568
  86.8 1.0 %copy.13 = bf16[1,512,1024]{2,1,0:T(8,128)(2,1)} copy(bf16[1,512,1024]{2,1,0:T(8,128)(2,1)S(1)} %bitcast.7) | data formatting | bytes 2097152
Async XLA Ops:
  0.0 0.8 copy-start
  0.8 0.7 copy-start.1
  1.5 0.7 copy-start.2
  2.2 0.7 copy-start.3
  2.9 0.7 copy-start.4
  3.6 0.7 copy-start.5
  4.3 0.7 copy-start.6

commit v5 on v4

--- a/solution.py
+++ b/solution.py
@@ -7,6 +7,7 @@
 from jax.experimental.pallas import tpu as pltpu
 from jax.sharding import PartitionSpec as P
 
+FIRST = 6
 MESH = pl.DeviceIdType.MESH
 F32 = jnp.float32
 BF16 = jnp.bfloat16
@@ -31,7 +32,6 @@
 LANES = 128
 COLS = C // LANES
 ROWS = 128
-WIN = 20
 SENDS = SHARDS - 1
 ALL_FRAMES = float(FRAMES * SHARDS * NX)
 NT = (((1,), (1,)), ((), ()))
@@ -53,7 +53,7 @@
     dw_ref,
     bn_gain_ref,
     bn_bias_ref,
-    out_ref,
+    out_hbm,
     enc,
     llm,
     w_in,
@@ -83,6 +83,7 @@
     d_pre,
     inc,
     d_mixed,
+    out_buf,
     ar_src,
     ar_s,
     ar_xy,
@@ -97,6 +98,7 @@
     halo_recv,
     ar_send,
     ar_recv,
+    out_sem,
     lines_in,
 ):
     sec = lax.axis_index("sec")
@@ -162,19 +164,22 @@
     tbl = pltpu.make_async_copy(row_buf.at[pl.ds(0, 1)], slot_tbl, tbl_sem.at[0])
     tbl.start()
     ids_line[z] = ids_row
-    loads[0].wait()
-    tbl.wait()
-
-    def pack(d, carry):
-        send[d] = llm[jnp.clip(slot_tbl[0, d], 0, 63)]
-        return carry
-
-    lax.fori_loop(0, SHARDS, pack, 0)
-    recv[me] = send[me]
 
     pl.semaphore_wait(barrier, len(greeted))
     for p in plane:
         pl.semaphore_signal(lines_in, inc=1, device_id=place(*p), device_id_type=MESH)
+    loads[0].wait()
+    tbl.wait()
+
+    def pack_to(to):
+        send[to] = llm[jnp.clip(slot_tbl[0, to], 0, 63)]
+
+    def pack(i):
+        s_at, z_at, y_at = partner(i)
+        pack_to(s_at * (NZ * NY) + z_at * NY + y_at)
+
+    for i in range(FIRST):
+        pack(i)
     pl.semaphore_wait(lines_in, len(plane))
 
     def spread(partners, source, target_of, s_sem, r_sem):
@@ -220,7 +225,7 @@
         return pltpu.make_async_remote_copy(
             send.at[to],
             recv.at[me],
-            a2a_send.at[lax.rem(i, WIN)],
+            a2a_send.at[i],
             a2a_recv,
             device_id=place(s_at, z_at, y_at, dp),
             device_id_type=MESH,
@@ -232,7 +237,6 @@
     def begin(count):
         low, high = started[0], min(SENDS, started[0] + count)
         started[0] = high
-        assert high - ended[0] <= WIN
 
         def step(i, carry):
             block_copy(i).start()
@@ -253,17 +257,24 @@
             lax.fori_loop(low, high, step, 0)
 
     def reserve(count):
-        first = (ended[0], started[0])
-        ended[0] += count
+        first = started[0]
         started[0] += count
         assert started[0] <= SENDS
         return first
 
     def pump(first, i):
-        block_copy(first[0] + i).wait_send()
-        block_copy(first[1] + i).start()
-
-    begin(6)
+        block_copy(first + i).start()
+
+    begin(FIRST)
+
+    def pack_more(i, carry):
+        for j in range(3):
+            pack(FIRST + 3 * i + j)
+        return carry
+
+    lax.fori_loop(0, (SENDS - FIRST) // 3, pack_more, 0)
+    recv[me] = llm[jnp.clip(slot_tbl[0, me], 0, 63)]
+    begin(10)
 
     gain = ln_gain_ref[...]
     bias = ln_bias_ref[...]
@@ -394,9 +405,8 @@
         for step, (partners, target) in enumerate(groups):
             wait_bytes(target.at[k, pl.ds(0, len(partners))], ar_send.at[k, step])
 
-    settle(4)
     sum_send(0, 0)
-    begin(7)
+    begin(4)
 
     wait_bytes(ids_line.at[pl.ds(0, NZ - 1)], ids_recv.at[0])
     for j in range(NZ):
@@ -406,13 +416,11 @@
     spread(plane, ids_tile, lambda i: ids_all.at[here], ids_send.at[1], ids_recv.at[1])
 
     sum_recv(0, 0)
-    settle(3)
     sum_send(0, 1)
     begin(14)
     sum_recv(0, 1)
-    settle(3)
     sum_send(0, 2)
-    begin(14)
+    begin(SENDS)
     sum_recv(0, 2)
 
     wait_bytes(ids_all.at[pl.ds(0, 7)], ids_recv.at[1])
@@ -424,7 +432,6 @@
     src_copy = pltpu.make_async_copy(row_buf.at[pl.ds(1, 1)], src_tbl, tbl_sem.at[1])
     src_copy.start()
 
-    moved_bn = reserve(8)
 
     def bn_scales(c):
         bn_mean = ar_src[0, 3, 0, pl.ds(c, 1), :] / ALL_FRAMES
@@ -455,15 +462,14 @@
                 z_total = z_total + weight * window[HALF + j : HALF + j + ROWS]
             ones_t[rows, cols] = ones_total
             z_t[rows, cols] = z_total
-        pump(moved_bn, c)
         return carry
 
     lax.fori_loop(0, COLS, normalise, 0)
     src_copy.wait()
     loads[3].wait()
-    settle(max(0, WIN - (SENDS - started[0])))
-    begin(SENDS)
     assert started[0] == SENDS
+
+    settle(8)
 
     wait_bytes(recv.at[pl.ds(0, SENDS)], a2a_recv)
 
@@ -532,18 +538,24 @@
 
     lax.fori_loop(0, COLS, assemble, 0)
 
+    stores = []
     for m in range(2):
-        rows = slice(m * 256, m * 256 + 256)
-        h = lax.dot_general(d_mixed[rows, :], w_in[...], NT, preferred_element_type=F32)
-        h = h * gain
-        hat = x_hat[rows, :]
+        part = slice(m * 256, m * 256 + 256)
+        h = lax.dot_general(d_mixed[part, :], w_in[...], NT, preferred_element_type=F32) * gain
+        hat = x_hat[part, :]
         mean = jnp.mean(h, axis=1, keepdims=True)
         along = jnp.mean(h * hat, axis=1, keepdims=True)
-        scale = rstd[rows, 0:1]
-        out_ref[rows, :] = (inc[rows, :].astype(F32) + scale * (h - mean - hat * along)).astype(BF16)
+        scale = rstd[part, 0:1]
+        out_buf[part, :] = (inc[part, :].astype(F32) + scale * (h - mean - hat * along)).astype(BF16)
+        at = pl.ds(m * 256, 256)
+        store = pltpu.make_async_copy(out_buf.at[at], out_hbm.at[at], out_sem.at[m])
+        store.start()
+        stores.append(store)
 
     edges_out(d_pre, PAD, 1)
     sum_done(1)
+    for store in stores:
+        store.wait()
 
 
 def local(
@@ -560,7 +572,7 @@
     w_out,
 ):
     vmem = pl.BlockSpec(memory_space=pltpu.VMEM)
-    hbm = pl.BlockSpec(memory_space=pltpu.HBM)
+    hbm = pl.BlockSpec(memory_space=pl.ANY)
     dma = pltpu.SemaphoreType.DMA
     full = pltpu.VMEM((FRAMES, C), F32)
     wide = pltpu.VMEM((EXT, C), F32)
@@ -569,7 +581,7 @@
         kernel,
         out_shape=jax.ShapeDtypeStruct((FRAMES, C), BF16),
         in_specs=[hbm] * 4 + [vmem] * 7,
-        out_specs=vmem,
+        out_specs=hbm,
         scratch_shapes=[
             pltpu.VMEM((WIDE, C), BF16),
             blocks,
@@ -600,13 +612,14 @@
             wide,
             pltpu.VMEM((FRAMES, C), BF16),
             pltpu.VMEM((FRAMES, 2 * C), BF16),
+            pltpu.VMEM((FRAMES, C), BF16),
             pltpu.VMEM((2, 4, 2, COLS, LANES), F32),
             pltpu.VMEM((2, 1, 2, COLS, LANES), F32),
             pltpu.VMEM((2, 15, 2, COLS, LANES), F32),
             pltpu.VMEM((2, 7, 2, COLS, LANES), F32),
             dma((4,)),
             dma((2,)),
-            dma((WIN,)),
+            dma((SENDS,)),
             dma,
             dma((2,)),
             dma((2,)),
@@ -614,10 +627,11 @@
             dma((2, 2)),
             dma((2, 3)),
             dma((2, 3)),
+            dma((4,)),
             pltpu.SemaphoreType.REGULAR,
         ],
         compiler_params=pltpu.CompilerParams(
-            collective_id=1, has_side_effects=True, vmem_limit_bytes=52 << 20
+            collective_id=1, has_side_effects=True, vmem_limit_bytes=56 << 20
         ),
         name="conv_module_back",
     )(

time: 88.1 us -> 81.8 us (0.928)
  local copies, waits for them, and re-layouts: 5.89 us -> 2.26 us
  Pallas kernels: 81.9 us -> 79.4 us
    unnamed x15 -> x1, local copies, waits for them, and re-layouts: 5.89 us -> 2.26 us
    pallas_call x1, Pallas kernels: 81.9 us -> 79.4 us  [local(): pl.pallas_call(kernel, out_shape=jax.ShapeDtypeStruct((FRAMES, C), BF16),...]
where the time goes in v5:
time: 81.8 us; the launch traced here: 81.7 us
  Pallas kernels  79.4 us (97%)
  local copies, waits for them, and re-layouts  2.26 us (3%)
    pallas_call x1, Pallas kernels, local(): pl.pallas_call(kernel, out_shape=jax.ShapeDtypeStruct((FRAMES, C), BF16),...  79.4 us
    unnamed x1, local copies, waits for them, and re-layouts  2.26 us

profile of v5, /device:TPU:1, one launch (start us, length us, event | category | flops | bytes accessed | tf_op | source)
XLA Modules:
  0.0 81.7 jit_solution(8970460288128497988)
XLA Ops:
  0.0 79.4 %conv_module_back.1 = bf16[512,1024]{1,0:T(8,128)(2,1)} custom-call(bf16[512,1024]{1,0:T(8,128)(2,1)} %bitcast.9, bf16[64,16,1024]{2,1,0:T(8,128)(2,1)} %bitcast.8, bf16[1024,2048]{1,0:T(8,128)(2,1)} %w_in_hbm.1, bf16[1024,1024]{1,0:T(8,128)(2,1)} %w_out_hbm.1, s32[1,64]{1,0:T(1,128)} %slot_ref.1, s32[1,262]{1,0:T(1,128)} %utt_ref.1, f32[1,1024]{1,0:T(1,128)} %bitcast.10, ...), custom_call_target="tpu_custom_call" | custom-call | tf_op jit(solution)/shard_map/conv_module_back/pallas_call | solution.py:580
  79.4 2.3 %copy.13 = bf16[1,512,1024]{2,1,0:T(8,128)(2,1)} copy(bf16[1,512,1024]{2,1,0:T(8,128)(2,1)} %bitcast.7) | data formatting | bytes 2097152

commit v6 on v5

--- a/solution.py
+++ b/solution.py
@@ -8,6 +8,7 @@
 from jax.sharding import PartitionSpec as P
 
 FIRST = 6
+SMALL = 16
 MESH = pl.DeviceIdType.MESH
 F32 = jnp.float32
 BF16 = jnp.bfloat16
@@ -46,14 +47,9 @@
     llm_hbm,
     w_in_hbm,
     w_out_hbm,
-    slot_ref,
-    utt_ref,
-    ln_gain_ref,
-    ln_bias_ref,
-    dw_ref,
-    bn_gain_ref,
-    bn_bias_ref,
-    out_hbm,
+    small,
+    ints,
+    out_ref,
     enc,
     llm,
     w_in,
@@ -66,7 +62,6 @@
     ids_line,
     ids_tile,
     ids_all,
-    utt_pad,
     seg,
     masks,
     x_hat,
@@ -83,7 +78,6 @@
     d_pre,
     inc,
     d_mixed,
-    out_buf,
     ar_src,
     ar_s,
     ar_xy,
@@ -98,7 +92,6 @@
     halo_recv,
     ar_send,
     ar_recv,
-    out_sem,
     lines_in,
 ):
     sec = lax.axis_index("sec")
@@ -150,7 +143,7 @@
     for p in greeted:
         pl.semaphore_signal(barrier, inc=1, device_id=place(*p), device_id_type=MESH)
 
-    slot_row = slot_ref[...]
+    slot_row = ints[:, UTT_PAD : UTT_PAD + 64]
     lane = lax.broadcasted_iota(I32, (64, LANES), 1)
     sub = lax.broadcasted_iota(I32, (64, LANES), 0)
     lane64 = lax.broadcasted_iota(I32, (64, 64), 1)
@@ -276,8 +269,8 @@
     recv[me] = llm[jnp.clip(slot_tbl[0, me], 0, 63)]
     begin(10)
 
-    gain = ln_gain_ref[...]
-    bias = ln_bias_ref[...]
+    gain = small[9:10, :]
+    bias = small[10:11, :]
 
     def norm_rows(values):
         values = values.astype(F32)
@@ -298,9 +291,7 @@
 
     lax.fori_loop(0, 8, norm, 0)
 
-    utt_pad[...] = jnp.zeros((8, UTT_PAD), I32)
-    utt_pad[0:1, 0:UTT] = utt_ref[...]
-    lengths = utt_pad[...].astype(F32).astype(BF16)
+    lengths = jnp.broadcast_to(ints[:, 0:UTT_PAD].astype(F32), (8, UTT_PAD)).astype(BF16)
     upper = (
         lax.broadcasted_iota(I32, (UTT_PAD, UTT_PAD), 0)
         <= lax.broadcasted_iota(I32, (UTT_PAD, UTT_PAD), 1)
@@ -354,7 +345,7 @@
 
     def convolve(c, carry):
         cols = pl.ds(pl.multiple_of(c * LANES, LANES), LANES)
-        taps = dw_ref[:, cols]
+        taps = small[0:TAPS, cols]
         first_sum = jnp.zeros((1, LANES), F32)
         second_sum = jnp.zeros((1, LANES), F32)
         for r in range(EXT // THIRD):
@@ -441,9 +432,9 @@
     def normalise(c, carry):
         cols = pl.ds(pl.multiple_of(c * LANES, LANES), LANES)
         bn_mean, bn_rstd = bn_scales(c)
-        bn_gain = bn_gain_ref[pl.ds(c, 1), :]
-        bn_bias = bn_bias_ref[pl.ds(c, 1), :]
-        taps = dw_ref[:, cols]
+        bn_gain = small[11:12, cols]
+        bn_bias = small[12:13, cols]
+        taps = small[0:TAPS, cols]
         factor = bn_gain * bn_rstd
         for r in range(EXT // 48):
             rows = slice(r * 48, r * 48 + 48)
@@ -494,8 +485,8 @@
     def conv_back(c, carry):
         cols = pl.ds(pl.multiple_of(c * LANES, LANES), LANES)
         bn_mean, bn_rstd = bn_scales(c)
-        factor = bn_gain_ref[pl.ds(c, 1), :] * bn_rstd
-        taps = dw_ref[:, cols] * factor
+        factor = small[11:12, cols] * bn_rstd
+        taps = small[0:TAPS, cols] * factor
         for r in range(FRAMES // ROWS):
             rows = slice(r * ROWS, r * ROWS + ROWS)
             window = d_pre[r * ROWS : r * ROWS + ROWS + 2 * PAD, cols]
@@ -538,7 +529,6 @@
 
     lax.fori_loop(0, COLS, assemble, 0)
 
-    stores = []
     for m in range(2):
         part = slice(m * 256, m * 256 + 256)
         h = lax.dot_general(d_mixed[part, :], w_in[...], NT, preferred_element_type=F32) * gain
@@ -546,16 +536,10 @@
         mean = jnp.mean(h, axis=1, keepdims=True)
         along = jnp.mean(h * hat, axis=1, keepdims=True)
         scale = rstd[part, 0:1]
-        out_buf[part, :] = (inc[part, :].astype(F32) + scale * (h - mean - hat * along)).astype(BF16)
-        at = pl.ds(m * 256, 256)
-        store = pltpu.make_async_copy(out_buf.at[at], out_hbm.at[at], out_sem.at[m])
-        store.start()
-        stores.append(store)
+        out_ref[part, :] = (inc[part, :].astype(F32) + scale * (h - mean - hat * along)).astype(BF16)
 
     edges_out(d_pre, PAD, 1)
     sum_done(1)
-    for store in stores:
-        store.wait()
 
 
 def local(
@@ -577,11 +561,21 @@
     full = pltpu.VMEM((FRAMES, C), F32)
     wide = pltpu.VMEM((EXT, C), F32)
     blocks = pltpu.VMEM((SHARDS, BLK, C), BF16)
+    def row(values, at):
+        values = values.reshape(-1, C)
+        return jnp.pad(values, ((at, SMALL - at - values.shape[0]), (0, 0)))
+
+    small = row(dw_kernel, 0)
+    for at, values in enumerate((ln_gain, ln_bias, bn_gain, bn_bias), TAPS):
+        small = small + row(values, at)
+    ints = jnp.concatenate(
+        [jnp.pad(utt_lengths, ((0, 0), (0, UTT_PAD - UTT))), jnp.pad(slot_block, ((0, 0), (0, 64)))], axis=1
+    )
     out = pl.pallas_call(
         kernel,
         out_shape=jax.ShapeDtypeStruct((FRAMES, C), BF16),
-        in_specs=[hbm] * 4 + [vmem] * 7,
-        out_specs=hbm,
+        in_specs=[hbm] * 4 + [vmem] * 2,
+        out_specs=vmem,
         scratch_shapes=[
             pltpu.VMEM((WIDE, C), BF16),
             blocks,
@@ -595,7 +589,6 @@
             pltpu.VMEM((NZ, 1, LANES), I32),
             pltpu.VMEM((NZ, LANES), I32),
             pltpu.VMEM((8, NZ, LANES), I32),
-            pltpu.VMEM((8, UTT_PAD), I32),
             pltpu.VMEM((WIDE, LANES), F32),
             pltpu.VMEM((TAPS, EXT, LANES), F32),
             full,
@@ -612,7 +605,6 @@
             wide,
             pltpu.VMEM((FRAMES, C), BF16),
             pltpu.VMEM((FRAMES, 2 * C), BF16),
-            pltpu.VMEM((FRAMES, C), BF16),
             pltpu.VMEM((2, 4, 2, COLS, LANES), F32),
             pltpu.VMEM((2, 1, 2, COLS, LANES), F32),
             pltpu.VMEM((2, 15, 2, COLS, LANES), F32),
@@ -627,11 +619,10 @@
             dma((2, 2)),
             dma((2, 3)),
             dma((2, 3)),
-            dma((4,)),
             pltpu.SemaphoreType.REGULAR,
         ],
         compiler_params=pltpu.CompilerParams(
-            collective_id=1, has_side_effects=True, vmem_limit_bytes=56 << 20
+            collective_id=1, has_side_effects=True, vmem_limit_bytes=52 << 20
         ),
         name="conv_module_back",
     )(
@@ -639,13 +630,8 @@
         llm_grads[0].reshape(SHARDS, BLK, C),
         w_in,
         w_out,
-        slot_block,
-        utt_lengths,
-        ln_gain.reshape(1, C),
-        ln_bias.reshape(1, C),
-        dw_kernel,
-        bn_gain.reshape(COLS, LANES),
-        bn_bias.reshape(COLS, LANES),
+        small,
+        ints,
     )
     return out[None]
 

time: 81.8 us -> 80.5 us (0.984)
  other arithmetic: 0 us -> 1.63 us
  Pallas kernels: 79.4 us -> 77.8 us
  local copies, waits for them, and re-layouts: 2.26 us -> 0.97 us
    pallas_call x1, Pallas kernels: 79.4 us -> 77.8 us  [local(): pl.pallas_call(kernel, out_shape=jax.ShapeDtypeStruct((FRAMES, C), BF16),...]
    unnamed x1, local copies, waits for them, and re-layouts: 2.26 us -> 0.97 us
    add x0 -> x1, other arithmetic: none -> 0.93 us  [local(): small = small + row(values, at)]
where the time goes in v6:
time: 80.5 us; the launch traced here: 80.4 us
  Pallas kernels  77.8 us (97%)
  other arithmetic  1.63 us (2%)
  local copies, waits for them, and re-layouts  0.97 us (1%)
    pallas_call x1, Pallas kernels, local(): pl.pallas_call(kernel, out_shape=jax.ShapeDtypeStruct((FRAMES, C), BF16),...  77.8 us

profile of v6, /device:TPU:1, one launch (start us, length us, event | category | flops | bytes accessed | tf_op | source)
XLA Modules:
  0.0 80.4 jit_solution(12904749563929817731)
XLA Ops:
  0.0 0.7 pad_add_fusion.1.ints
  0.7 0.9 %pad_add_fusion.small = f32[16,1024]{1,0:T(8,128)S(1)} fusion(f32[1,1024]{1,0:T(1,128)} %bitcast.10, f32[1,1024]{1,0:T(1,128)} %bitcast.11, f32[1,1024]{1,0:T(1,128)} %bitcast.12, f32[1,1024]{1,0:T(1,128)} %bitcast.13, f32[9,1024]{1,0:T(8,128)} %param.18), kind=kLoop, calls=%fused_computation | loop fusion | flops 65536 | bytes 118784 | tf_op jit(solution)/shard_map/add | solution.py:570
  1.6 77.8 %conv_module_back.1 = bf16[512,1024]{1,0:T(8,128)(2,1)S(1)} custom-call(bf16[512,1024]{1,0:T(8,128)(2,1)} %bitcast.9, bf16[64,16,1024]{2,1,0:T(8,128)(2,1)} %bitcast.8, bf16[1024,2048]{1,0:T(8,128)(2,1)} %w_in_hbm.1, bf16[1024,1024]{1,0:T(8,128)(2,1)} %w_out_hbm.1, f32[16,1024]{1,0:T(8,128)S(1)} %pad_add_fusion.small, s32[1,512]{1,0:T(1,128)S(1)} %pad_add_fusion.1.ints), custom_call_target="tpu_custom_call" | custom-call | tf_op jit(solution)/shard_map/conv_module_back/pallas_call | solution.py:574
  79.4 1.0 %copy.13 = bf16[1,512,1024]{2,1,0:T(8,128)(2,1)} copy(bf16[1,512,1024]{2,1,0:T(8,128)(2,1)S(1)} %bitcast.7) | data formatting | bytes 2097152
